TPU v7x, 32 devices: a whole 2x2x4 slice. The times are simulated.
32 devices in a mesh: fsdp: 2 (over y), seq: 16 (over z, x, core).
Axes of the slice: x: 2, y: 2, z: 4, core: 2. Of those that a mesh axis runs over, the one named last changes fastest.
Arguments:
- inputs: bfloat16 [2, 2, 1024, 2560], P(None, 'fsdp', 'seq'), may hold values from -26 to 26
- cotangent: bfloat16 [2, 2, 1024, 2560], P(None, 'fsdp', 'seq'), may hold values from -6 to 6
- proj_gelu: bfloat16 [2560, 2560], P(('fsdp', 'seq')), may hold values from -0.125 to 0.125
- proj_lru: bfloat16 [2560, 2560], P(('fsdp', 'seq')), may hold values from -0.125 to 0.125
- gate_blocks: bfloat16 [2560, 512], P(('fsdp', 'seq')), may hold values from -0.375 to 0.375
- proj_out: bfloat16 [2560, 2560], P(None, ('fsdp', 'seq')), may hold values from -0.125 to 0.125
- ffw_gate: bfloat16 [2560, 7680], P(('fsdp', 'seq')), may hold values from -0.125 to 0.125
- ffw_up: bfloat16 [2560, 7680], P(('fsdp', 'seq')), may hold values from -0.125 to 0.125
- ffw_down: bfloat16 [7680, 2560], P(None, ('fsdp', 'seq')), may hold values from -0.0625 to 0.0625
- norm_mix: bfloat16 [2560], P(('fsdp', 'seq')), may hold values from 0.099609375 to 1.8984375
- norm_ffw: bfloat16 [2560], P(('fsdp', 'seq')), may hold values from 0.099609375 to 1.8984375
- decay_param: bfloat16 [2560], P(('fsdp', 'seq')), may hold values from 4 to 14
- conv_taps: bfloat16 [2560, 4], P(('fsdp', 'seq')), may hold values from -2.5 to 2.5
Outputs:
- mixed_out: bfloat16 [2, 2, 1024, 2560], P(None, 'fsdp', 'seq')
- grad_inputs: float32 [2, 2, 1024, 2560], P(None, 'fsdp', 'seq')
- grad_proj_gelu: float32 [2560, 2560], P(('fsdp', 'seq'))
- grad_proj_lru: float32 [2560, 2560], P(('fsdp', 'seq'))
- grad_gate_blocks: float32 [2560, 512], P(('fsdp', 'seq'))
- grad_proj_out: float32 [2560, 2560], P(None, ('fsdp', 'seq'))
- grad_ffw_gate: float32 [2560, 7680], P(('fsdp', 'seq'))
- grad_ffw_up: float32 [2560, 7680], P(('fsdp', 'seq'))
- grad_ffw_down: float32 [7680, 2560], P(None, ('fsdp', 'seq'))
- grad_norm_mix: float32 [2560], P(('fsdp', 'seq'))
- grad_norm_ffw: float32 [2560], P(('fsdp', 'seq'))
- grad_decay_param: float32 [2560], P(('fsdp', 'seq'))
- grad_conv_taps: float32 [2560, 4], P(('fsdp', 'seq'))
All inputs are finite; a program needn't handle non-finite values.
Results may differ from a plain program's by a relative error of at most 0.009.
Values may be sent and summed in bfloat16 or wider, within the bound.
A program may use at most 1 GiB of HBM per device.

v0:
```python
import functools

import jax
import jax.numpy as jnp
from jax import lax
from jax.experimental import pallas as pl
from jax.experimental.pallas import tpu as pltpu
from jax.sharding import PartitionSpec as P

EPS = 1e-06
GUARD = 0.001
RATE = 8.0
TP = 4
NQ = 4
HALO = 8
BF = jnp.bfloat16
F32 = jnp.float32
MESH = pl.DeviceIdType.MESH
ANY = pl.BlockSpec(memory_space=pl.ANY)
VMEM = pl.BlockSpec(memory_space=pltpu.VMEM)
GRANT = 60 * 1024 * 1024
CUTS = 2
FREE = pl.CostEstimate(flops=0, bytes_accessed=0, transcendentals=0)


def move(value, step):
    pairs = []
    for here in range(lax.axis_size("seq")):
        there = step(here // (TP * NQ), here // NQ % TP, here % NQ)
        if there is not None:
            pairs.append((here, (there[0] * TP + there[1]) * NQ + there[2]))
    return lax.ppermute(value, "seq", pairs)


def swap_core(value):
    return move(value, lambda r, z, q: (r, z, q ^ 1))


def swap_x(value):
    return move(value, lambda r, z, q: (r, z, q ^ 2))


def swap_f(value):
    return lax.ppermute(value, "fsdp", [(0, 1), (1, 0)])


def shift_z(value, d):
    return move(value, lambda r, z, q: (r, (z + d) % TP, q))


def shift_q(value, d):
    return move(value, lambda r, z, q: (r, z, (q + d) % NQ))


def shift_r(value, d):
    count = lax.axis_size("seq") // (TP * NQ)
    return move(value, lambda r, z, q: ((r + d) % count, z, q))


def hop(value, d, low, high):
    return move(value, lambda r, z, q: (r, z + d, q) if low <= z <= high else None)


class Place:
    def __init__(self):
        seq = lax.axis_index("seq")
        self.f = lax.axis_index("fsdp")
        self.r, self.z, self.q = seq // (TP * NQ), seq // NQ % TP, seq % NQ
        self.x, self.c = self.q // 2, self.q % 2
        self.rests = lax.axis_size("seq") // (TP * NQ)
        self.fs = lax.axis_size("fsdp")
        self.index = self.f * lax.axis_size("seq") + seq


def at(value, index):
    return lax.dynamic_index_in_dim(value, index, 0, keepdims=False)


def put(base, value, *index):
    starts = [jnp.int32(0) if i is None else jnp.int32(i) for i in index]
    starts += [jnp.int32(0)] * (base.ndim - len(index))
    for dim, i in enumerate(index):
        if i is not None:
            value = jnp.expand_dims(value, dim)
    return lax.dynamic_update_slice(base, value, starts)


def everywhere(value, shifter, mine, count):
    out = put(jnp.zeros((count,) + value.shape, value.dtype), value, mine)
    for d in range(1, count):
        out = put(out, shifter(value, d), (mine - d) % count)
    return out


def gather_z(value, p):
    ups, downs = [], []
    up = down = value
    for k in range(1, TP):
        up = hop(up, 1, k - 1, TP - 2)
        down = hop(down, -1, 1, TP - k)
        ups.append(up)
        downs.append(down)
    out = put(jnp.zeros((TP,) + value.shape, value.dtype), value, p.z)
    for k in range(1, TP):
        out = put(out, downs[k - 1] + ups[TP - 1 - k], (p.z + k) % TP)
    return out


def scatter_z(parts, p):
    right = left = None
    for k in range(TP - 1, 0, -1):
        send = at(parts, (p.z + k) % TP)
        if right is not None:
            send = (send.astype(F32) + right.astype(F32)).astype(BF)
        right = hop(send, 1, 0, TP - 1 - k)
        send = at(parts, (p.z - k) % TP)
        if left is not None:
            send = (send.astype(F32) + left.astype(F32)).astype(BF)
        left = hop(send, -1, k, TP - 1)
    return at(parts, p.z).astype(F32) + right.astype(F32) + left.astype(F32)


def weights_in(pieces, p):
    rows, cols = pieces.shape[1:]
    mine = put(jnp.zeros(pieces.shape, BF), at(pieces, p.z), p.z)
    for d in range(1, TP):
        mine = put(mine, shift_z(at(pieces, (p.z + d) % TP), d), (p.z - d) % TP)
    mine = everywhere(mine, shift_r, p.r, p.rests)
    half = TP // 2
    by_x, by_f = swap_x(mine), swap_f(mine)
    corner = (swap_f(by_x[:, :half]), swap_x(by_f[:, half:]))
    whole = jnp.zeros((p.fs, p.rests, TP, 2, 2, rows, cols), BF)
    for block, f, x, z in (
        (mine, p.f, p.x, 0),
        (by_x, p.f, 1 - p.x, 0),
        (by_f, 1 - p.f, p.x, 0),
        (corner[0], 1 - p.f, 1 - p.x, 0),
        (corner[1], 1 - p.f, 1 - p.x, half),
    ):
        other = swap_core(block)
        for part, c in ((block, p.c), (other, 1 - p.c)):
            part = part[None, :, :, None, None]
            whole = lax.dynamic_update_slice(
                whole, part, [jnp.int32(i) for i in (f, 0, z, x, c, 0, 0)]
            )
    return whole.reshape(-1, cols)


def by_owner(grad, p):
    return grad.reshape(p.fs, p.rests, TP, 2, 2, -1, grad.shape[1])


def to_owner_z(total, p):
    out = put(jnp.zeros(total.shape, BF), at(total, p.z), p.z)
    for d in (1, 3, 2):
        out = put(out, shift_z(at(total, (p.z + d) % TP), d), (p.z - d) % TP)
    return out


def grads_out(grad, p):
    plus = lambda a, b: (a.astype(F32) + b.astype(F32)).astype(BF)
    pick = lambda v, dim, i: lax.dynamic_index_in_dim(v, i, dim, keepdims=False)
    total = by_owner(grad, p)
    total = plus(pick(total, 4, p.c), swap_core(pick(total, 4, 1 - p.c)))
    total = plus(pick(total, 3, p.x), swap_x(pick(total, 3, 1 - p.x)))
    total = plus(at(total, p.f), swap_f(at(total, 1 - p.f)))
    mine = at(total, p.r)
    for d in range(1, p.rests):
        mine = plus(mine, shift_r(at(total, (p.r + d) % p.rests), d))
    return to_owner_z(mine, p)


def dot_left_t(left_mat, right_mat):
    return lax.dot_general(
        left_mat, right_mat, (((0,), (0,)), ((), ())), preferred_element_type=F32
    )


def dot_plain(left_mat, right_mat):
    return jnp.dot(left_mat, right_mat, preferred_element_type=F32)


def dot_right_t(left_mat, right_mat):
    return lax.dot_general(
        left_mat, right_mat, (((1,), (1,)), ((), ())), preferred_element_type=F32
    )


def normed(values, gain_vec):
    return values * lax.rsqrt(jnp.mean(values * values, axis=-1, keepdims=True) + EPS) * gain_vec


def gelu_pair(v):
    scale = 0.7978845608028654
    inner = jnp.tanh(scale * (v + 0.044715 * v * v * v))
    slope = 0.5 * v * (1.0 - inner * inner) * scale * (1.0 + 0.134145 * v * v)
    return 0.5 * v * (1.0 + inner), 0.5 * (1.0 + inner) + slope


def span_scan(decay, drive, backward):
    count = decay.shape[0]
    row = lax.broadcasted_iota(jnp.int32, decay.shape, 0)
    step = 1
    while step < count:
        inside = row < count - step if backward else row >= step
        turn = count - step if backward else step
        drive = drive + jnp.where(inside, decay * pltpu.roll(drive, turn, 0), 0.0)
        decay = decay * jnp.where(inside, pltpu.roll(decay, turn, 0), 1.0)
        step *= 2
    return decay, drive


def gate_values(gate, soft):
    half = gate.shape[1] // 2
    rec_gate = jax.nn.sigmoid(gate[:, :half])
    in_gate = jax.nn.sigmoid(gate[:, half:])
    log_decay = -RATE * rec_gate * soft
    square = jnp.exp(2.0 * log_decay)
    return rec_gate, in_gate, jnp.exp(log_decay), square, jnp.sqrt(1.0 - square + GUARD)


def main_rows(i, span, micro):
    return pl.ds(i // micro * micro * (span + HALO) + i % micro * span, span)


def with_halo(pre, i, span, micro):
    start = i // micro * micro * (span + HALO) + micro * span + i % micro * HALO
    both = [pre[pl.ds(start, HALO)], pre[main_rows(i, span, micro)]]
    return jnp.concatenate(both, axis=0)


def recur_head(span, micro, pre, rows, block, conv, gate, state, prod, sums):
    count = conv.shape[0] // span
    soft, taps = rows[0:1], [rows[k + 2 : k + 3] for k in range(4)]
    for i in range(count):
        vals = with_halo(pre, i, span, micro).astype(BF).astype(F32)
        total = taps[0] * vals
        for k in range(1, 4):
            total = total + taps[k] * pltpu.roll(vals, k, 0)
        conv[pl.ds(i * span, span)] = total[HALO:].astype(BF)
    gate[...] = dot_plain(conv[...], block[...])
    for i in range(count):
        here = pl.ds(i * span, span)
        _, in_gate, decay, _, root = gate_values(gate[here], soft)
        decay, local = span_scan(decay, root * in_gate * conv[here].astype(F32), False)
        state[here] = local
        prod[here] = decay
        sums[0, i : i + 1] = decay[span - 1 :]
        sums[1, i : i + 1] = local[span - 1 :]


def columns(ref, h, width):
    return ref.at[:, pl.ds(pl.multiple_of(h * width, 128), width)]


def by_heads(count, body):
    def turn(h, _):
        body(h)
        return 0

    lax.fori_loop(0, count, turn, 0)


def recur_kernel(
    dims, x_all, mix_w, small, rows, mixed, pre, conv, gate, state, prod, sums,
    small_w, gl_w, block_w, mixed_all, sems,
):
    span, micro, heads, held, bw, taps = dims
    part = held * bw
    p = Place()
    start = pl.multiple_of(p.z * heads // TP * bw, 128)
    pieces = (
        (mix_w.at[:, pl.ds(3 * part + 2 * bw, 128)], small_w),
        (mix_w.at[:, pl.ds(0, 2 * part)], gl_w),
        (mix_w.at[pl.ds(start, part), pl.ds(3 * part, 2 * bw)], block_w),
    )
    loads = [pltpu.make_async_copy(src, dst, sems.at[i]) for i, (src, dst) in enumerate(pieces)]
    for load in loads:
        load.start()
    loads[0].wait()
    row = lax.broadcasted_iota(jnp.int32, (8, 128), 0)
    lane = lax.broadcasted_iota(jnp.int32, (8, 128), 1)
    small[...] = dot_right_t(jnp.where(row == lane, 1.0, 0.0).astype(BF), small_w[...])
    own = small[:, pl.ds(start, part)]
    decay = -own[2:3]
    feature = lax.broadcasted_iota(jnp.int32, (1, part), 1)
    count = ((p.z + 1) * heads // TP - p.z * heads // TP) * bw
    rows[0:1] = jnp.maximum(decay, 0.0) + jnp.log1p(jnp.exp(-jnp.abs(decay)))
    rows[1:2] = jax.nn.sigmoid(decay)
    rows[2 : 2 + taps] = own[3 : 3 + taps]
    rows[6:7] = jnp.where(feature < count, 1.0, 0.0)
    rows[7:8] = jnp.zeros((1, part), F32)
    gain, wide, step = small[0:1], micro * (span + HALO), 16

    def norm(z, _):
        for k in range(0, wide, step):
            vals = x_all[pl.ds(pl.multiple_of(z * wide + k, step), step)].astype(F32)
            vals = normed(vals, gain).astype(BF)
            mixed_all[pl.ds(pl.multiple_of(z * wide + k, step), step)] = vals
            if k < micro * span:
                mixed[pl.ds(pl.multiple_of(z * micro * span + k, step), step)] = vals
        return 0

    lax.fori_loop(0, TP, norm, 0)
    loads[1].wait()

    def project(h):
        cols = pl.ds(pl.multiple_of(h * bw, 128), bw)
        pre[:, cols] = dot_plain(mixed_all[...], gl_w[:, cols])

    by_heads(2 * held, project)
    loads[2].wait()

    def one_head(h):
        block = block_w.at[pl.ds(pl.multiple_of(h * bw, 128), bw)]
        sums_h = sums.at[:, :, pl.ds(pl.multiple_of(h * bw, 128), bw)]
        recur_head(
            span, micro, columns(pre, held + h, bw), columns(rows, h, bw), block,
            columns(conv, h, bw), columns(gate, h, 2 * bw), columns(state, h, bw),
            columns(prod, h, bw), sums_h,
        )

    by_heads(held, one_head)


def recur(x_all, mix_w, dims):
    span, micro, _, held, bw, _ = dims
    part, width = held * bw, x_all.shape[1]
    tokens = x_all.shape[0] // (span + HALO) * span
    shapes = [((8, width), F32), ((8, part), F32), ((tokens, width), BF)]
    shapes += [((x_all.shape[0], 2 * part), F32), ((tokens, part), BF), ((tokens, 2 * part), F32)]
    shapes += [((tokens, part), F32), ((tokens, part), F32), ((2, tokens // span, part), F32)]
    return pl.pallas_call(
        functools.partial(recur_kernel, dims),
        in_specs=[VMEM, ANY],
        out_specs=[VMEM] * len(shapes),
        out_shape=[jax.ShapeDtypeStruct(*shape) for shape in shapes],
        scratch_shapes=[
            pltpu.VMEM((width, 128), BF),
            pltpu.VMEM((width, 2 * part), BF),
            pltpu.VMEM((part, 2 * bw), BF),
            pltpu.VMEM(x_all.shape, BF),
            pltpu.SemaphoreType.DMA((3,)),
        ],
        cost_estimate=FREE,
        compiler_params=pltpu.CompilerParams(vmem_limit_bytes=GRANT),
    )(x_all, mix_w)


def recur_mix_kernel(dims, pre, rows, state, prod, start, mix_w, mix, parts, out_w, sem):
    span, micro, _, held, bw, _ = dims
    part = held * bw
    load = pltpu.make_async_copy(mix_w.at[:, pl.ds(2 * part, part)], out_w, sem.at[0])
    load.start()

    def one_head(h):
        pre_h, state_h, prod_h = columns(pre, h, bw), columns(state, h, bw), columns(prod, h, bw)
        rows_h, start_h, mix_h = columns(rows, h, bw), columns(start, h, bw), columns(mix, h, bw)
        for i in range(state.shape[0] // span):
            here = pl.ds(i * span, span)
            act, _ = gelu_pair(pre_h[main_rows(i, span, micro)])
            states = state_h[here] + prod_h[here] * start_h[i : i + 1]
            mix_h[here] = (states * act * rows_h[6:7]).astype(BF)

    by_heads(held, one_head)
    load.wait()

    def project(j):
        cols = pl.ds(pl.multiple_of(j * 256, 256), 256)
        parts[:, cols] = dot_right_t(mix[...], out_w[cols]).astype(BF)

    by_heads(out_w.shape[0] // 256, project)


def recur_mix(pre, rows, state, prod, start, mix_w, dims):
    tokens, part = state.shape
    width = mix_w.shape[0]
    return pl.pallas_call(
        functools.partial(recur_mix_kernel, dims),
        in_specs=[VMEM] * 5 + [ANY],
        out_specs=[VMEM, VMEM],
        out_shape=[
            jax.ShapeDtypeStruct((tokens, part), BF),
            jax.ShapeDtypeStruct((tokens, width), BF),
        ],
        scratch_shapes=[pltpu.VMEM((width, part), BF), pltpu.SemaphoreType.DMA((1,))],
        cost_estimate=FREE,
        compiler_params=pltpu.CompilerParams(vmem_limit_bytes=GRANT),
    )(pre, rows, state, prod, start, mix_w)


def recur_back_kernel(
    dims, grad, pre, rows, state, prod, start, gate, mix_w, gelu, local, prods, sums, back, out_w, sem
):
    span, micro, _, held, bw, _ = dims
    part = held * bw
    load = pltpu.make_async_copy(mix_w.at[:, pl.ds(2 * part, part)], out_w, sem.at[0])
    load.start()
    load.wait()

    def one_head(h):
        back[...] = dot_plain(grad[...], out_w[:, pl.ds(pl.multiple_of(h * bw, 128), bw)])
        pre_h, state_h, prod_h = columns(pre, h, bw), columns(state, h, bw), columns(prod, h, bw)
        rows_h, start_h, gate_h = columns(rows, h, bw), columns(start, h, bw), columns(gate, h, 2 * bw)
        gelu_h, local_h = columns(gelu, h, bw), columns(local, h, bw)
        prods_h, sums_h = columns(prods, h, bw), columns(sums, h, bw)
        soft = rows_h[0:1]
        for i in range(back.shape[0] // span):
            here = pl.ds(i * span, span)
            act, slope = gelu_pair(pre_h[main_rows(i, span, micro)])
            states = state_h[here] + prod_h[here] * start_h[i : i + 1]
            gelu_h[here] = (back[here] * states * slope * rows_h[6:7]).astype(BF)
            _, _, decay, _, _ = gate_values(gate_h[here], soft)
            row = lax.broadcasted_iota(jnp.int32, decay.shape, 0)
            later = jnp.where(row < span - 1, pltpu.roll(decay, span - 1, 0), 1.0)
            later, adjoint = span_scan(later, back[here] * act, True)
            local_h[here] = adjoint
            prods_h[here] = later
            sums_h[i : i + 1] = decay[:1] * adjoint[:1]

    by_heads(held, one_head)


def recur_back(grad, pre, rows, state, prod, start, gate, mix_w, dims):
    tokens, part = state.shape
    shapes = [((tokens, part), BF), ((tokens, part), F32), ((tokens, part), F32), (start.shape, F32)]
    return pl.pallas_call(
        functools.partial(recur_back_kernel, dims),
        in_specs=[VMEM] * 7 + [ANY],
        out_specs=[VMEM] * 4,
        out_shape=[jax.ShapeDtypeStruct(*shape) for shape in shapes],
        scratch_shapes=[
            pltpu.VMEM((tokens, dims[4]), F32),
            pltpu.VMEM((mix_w.shape[0], part), BF),
            pltpu.SemaphoreType.DMA((1,)),
        ],
        cost_estimate=FREE,
        compiler_params=pltpu.CompilerParams(vmem_limit_bytes=GRANT),
    )(grad, pre, rows, state, prod, start, gate, mix_w)


def recur_grad_kernel(
    span, micro, local, prods, carried, state, prod, start, gate, conv, pre, rows, block,
    blocks_out, lru_out, spill_out, rows_out, gate_grad, conv_grad,
):
    count = local.shape[0] // span
    soft, sig, own = rows[0:1], rows[1:2], rows[6:7]
    taps = [rows[k + 2 : k + 3] for k in range(4)]
    width = local.shape[1]
    add_up = lambda v: jnp.sum(v, axis=0, keepdims=True)
    decay_sum = jnp.zeros((1, width), F32)
    for i in range(count):
        here = pl.ds(i * span, span)
        adjoint = local[here] + prods[here] * carried[i : i + 1]
        states = state[here] + prod[here] * start[i : i + 1]
        row = lax.broadcasted_iota(jnp.int32, states.shape, 0)
        earlier = jnp.where(row >= 1, pltpu.roll(states, 1, 0), start[i : i + 1])
        rec_gate, in_gate, decay, square, root = gate_values(gate[here], soft)
        conv_vals = conv[here].astype(F32)
        drive = adjoint * conv_vals
        grad_log = adjoint * earlier * decay - drive * in_gate * square / root
        decay_sum = decay_sum + add_up(grad_log * rec_gate)
        gate_grad[here, :width] = (-RATE * soft * grad_log * rec_gate * (1.0 - rec_gate)).astype(BF)
        gate_grad[here, width:] = (drive * root * in_gate * (1.0 - in_gate)).astype(BF)
        conv_grad[here] = adjoint * root * in_gate
    blocks_out[...] = lax.dot_general(
        conv[...], gate_grad[...], (((0,), (0,)), ((), ())), preferred_element_type=F32
    )
    conv_grad[...] += dot_right_t(gate_grad[...], block[0])
    tap_sums = [jnp.zeros((1, width), F32) for _ in range(4)]
    for i in range(count):
        here = pl.ds(i * span, span)
        grad = conv_grad[here]
        vals = with_halo(pre, i, span, micro).astype(BF).astype(F32)
        wide = jnp.concatenate([jnp.zeros((HALO, width), F32), grad], axis=0)
        total = taps[0] * wide
        tap_sums[0] = tap_sums[0] + add_up(grad * vals[HALO:])
        for k in range(1, 4):
            total = total + taps[k] * pltpu.roll(wide, span + HALO - k, 0)
            tap_sums[k] = tap_sums[k] + add_up(grad * pltpu.roll(vals, k, 0)[HALO:])
        lru_out[here] = total[HALO:]
        spill_out[pl.ds(i * HALO, HALO)] = total[:HALO]
    rows_out[...] = jnp.zeros(rows_out.shape, F32)
    rows_out[0:1] = decay_sum * sig * own * RATE
    for k in range(4):
        rows_out[k + 1 : k + 2] = tap_sums[k] * own


def recur_grad(local, prods, carried, state, prod, start, gate, conv, pre, rows, blocks, dims):
    tokens, part = state.shape
    span, micro, _, held, bw, _ = dims
    column = lambda h: (0, h)
    whole = pl.BlockSpec((tokens, bw), column)
    ends = pl.BlockSpec((start.shape[0], bw), column)
    return pl.pallas_call(
        functools.partial(recur_grad_kernel, span, micro),
        grid=(held,),
        in_specs=[
            whole,
            whole,
            ends,
            whole,
            whole,
            ends,
            pl.BlockSpec((tokens, 2 * bw), column),
            whole,
            pl.BlockSpec((pre.shape[0], bw), lambda h: (0, held + h)),
            pl.BlockSpec((8, bw), column),
            pl.BlockSpec((1, bw, 2 * bw), lambda h: (h, 0, 0)),
        ],
        out_specs=[
            pl.BlockSpec((bw, 2 * bw), lambda h: (h, 0)),
            whole,
            pl.BlockSpec((start.shape[0] * HALO, bw), column),
            pl.BlockSpec((8, bw), column),
        ],
        out_shape=[
            jax.ShapeDtypeStruct((part, 2 * bw), F32),
            jax.ShapeDtypeStruct((tokens, part), F32),
            jax.ShapeDtypeStruct((start.shape[0] * HALO, part), F32),
            jax.ShapeDtypeStruct((8, part), F32),
        ],
        scratch_shapes=[pltpu.VMEM((tokens, 2 * bw), BF), pltpu.VMEM((tokens, bw), F32)],
        cost_estimate=FREE,
        compiler_params=pltpu.CompilerParams(vmem_limit_bytes=GRANT),
    )(local, prods, carried, state, prod, start, gate, conv, pre, rows, blocks)


def recur_in_kernel(
    dims, gelu, lru, spill, rows, small, mixed, mix_w, pair, parts, gains, gl_w, sem
):
    span, _, _, held, bw, _ = dims
    part = held * bw
    load = pltpu.make_async_copy(mix_w.at[:, pl.ds(0, 2 * part)], gl_w, sem.at[0])
    load.start()
    pair[:, :part] = gelu[...]

    def one_head(h):
        lru_h, spill_h, own = columns(lru, h, bw), columns(spill, h, bw), columns(rows, h, bw)[6:7]
        for i in range(lru.shape[0] // span):
            vals = lru_h[pl.ds(i * span, span)]
            late = vals[span - HALO :] + spill_h[pl.ds(i * HALO, HALO)]
            vals = jnp.concatenate([vals[: span - HALO], late], axis=0) * own
            pair[pl.ds(i * span, span), pl.ds(pl.multiple_of((held + h) * bw, 128), bw)] = vals.astype(BF)

    by_heads(held, one_head)
    load.wait()

    def project(j):
        cols = pl.ds(pl.multiple_of(j * 256, 256), 256)
        grad = dot_right_t(pair[...], gl_w[cols])
        parts[:, cols] = grad.astype(BF)
        gain = jnp.sum(grad * mixed[:, cols].astype(F32), axis=0, keepdims=True)
        gains[0:1, cols] = gain / small[0:1, cols]

    by_heads(gl_w.shape[0] // 256, project)


def recur_in(gelu, lru, spill, rows, small, mixed, mix_w, dims):
    tokens, part = gelu.shape
    width = mix_w.shape[0]
    return pl.pallas_call(
        functools.partial(recur_in_kernel, dims),
        in_specs=[VMEM] * 6 + [ANY],
        out_specs=[VMEM] * 3,
        out_shape=[
            jax.ShapeDtypeStruct((tokens, 2 * part), BF),
            jax.ShapeDtypeStruct((tokens, width), BF),
            jax.ShapeDtypeStruct((8, width), F32),
        ],
        scratch_shapes=[pltpu.VMEM((width, 2 * part), BF), pltpu.SemaphoreType.DMA((1,))],
        cost_estimate=FREE,
        compiler_params=pltpu.CompilerParams(vmem_limit_bytes=GRANT),
    )(gelu, lru, spill, rows, small, mixed, mix_w)


def device(p, f=None, z=None, x=None, c=None):
    f, z = p.f if f is None else f, p.z if z is None else z
    x, c = p.x if x is None else x, p.c if c is None else c
    return (f, ((p.r * TP + z) * 2 + x) * 2 + c)


def copy_to(src, dst, sems, index, dev):
    return pltpu.make_async_remote_copy(
        src_ref=src,
        dst_ref=dst,
        send_sem=sems[0].at[index],
        recv_sem=sems[1].at[index],
        device_id=dev,
        device_id_type=MESH,
    )


def pairs(*shape):
    return [pltpu.SemaphoreType.DMA(shape), pltpu.SemaphoreType.DMA(shape)]


def greet(devices):
    barrier = pltpu.get_barrier_semaphore()
    for dev in devices:
        pl.semaphore_signal(barrier, inc=1, device_id=dev, device_id_type=MESH)
    pl.semaphore_wait(barrier, len(devices))


def by_rows(count, body, step=16):
    def turn(i, _):
        body(pl.ds(pl.multiple_of(i * step, step), step))
        return 0

    assert count % step == 0
    lax.fori_loop(0, count // step, turn, 0)


class Gather:
    def __init__(self, p, out, ups, downs):
        self.p, self.out, self.ups, self.downs = p, out, ups, downs
        self.up = device(p, z=jnp.minimum(p.z + 1, TP - 1))
        self.down = device(p, z=jnp.maximum(p.z - 1, 0))

    def begin(self, h, src):
        z = self.p.z

        @pl.when(z < TP - 1)
        def _():
            copy_to(src, self.out.at[z, h], self.ups, (0, h), self.up).start()

        @pl.when(z > 0)
        def _():
            copy_to(src, self.out.at[z, h], self.downs, (0, h), self.down).start()

    def step(self, k, h):
        z, out = self.p.z, self.out

        @pl.when(z >= k)
        def _():
            block = out.at[z - k, h]
            copy_to(block, block, self.ups, (k - 1, h), self.up).wait_recv()
            if k < TP - 1:

                @pl.when(z < TP - 1)
                def _():
                    copy_to(block, block, self.ups, (k, h), self.up).start()

        @pl.when(z <= TP - 1 - k)
        def _():
            block = out.at[z + k, h]
            copy_to(block, block, self.downs, (k - 1, h), self.down).wait_recv()
            if k < TP - 1:

                @pl.when(z > 0)
                def _():
                    copy_to(block, block, self.downs, (k, h), self.down).start()

    def close(self, halves):
        z, block = self.p.z, self.out.at[0, 0]
        for h in range(halves) if isinstance(halves, int) else halves:
            for k in range(TP - 1):

                @pl.when((z >= k) & (z < TP - 1))
                def _():
                    copy_to(block, block, self.ups, (k, h), self.up).wait_send()

                @pl.when((z <= TP - 1 - k) & (z > 0))
                def _():
                    copy_to(block, block, self.downs, (k, h), self.down).wait_send()


class LineSum:
    def __init__(self, p, parts, scratch):
        self.p, self.parts = p, parts
        self.got_up, self.got_down, self.out_up, self.out_down = scratch[:4]
        self.ups, self.downs = scratch[4:6], scratch[6:8]
        self.halves, self.rows = parts.shape[1:3]
        self.up = device(p, z=jnp.minimum(p.z + 1, TP - 1))
        self.down = device(p, z=jnp.maximum(p.z - 1, 0))

    @staticmethod
    def scratch(parts):
        block = parts[1:]
        return [
            pltpu.VMEM((TP - 1,) + block, BF),
            pltpu.VMEM((TP - 1,) + block, BF),
            pltpu.VMEM((TP - 2,) + block, BF),
            pltpu.VMEM((TP - 2,) + block, BF),
            *pairs(TP - 1, parts[1]),
            *pairs(TP - 1, parts[1]),
        ]

    def clear(self):
        z = self.p.z

        @pl.when(z == 0)
        def _():
            for h in range(self.halves):
                by_rows(self.rows, lambda at: self.fill(self.got_up, h, at))

        @pl.when(z == TP - 1)
        def _():
            for h in range(self.halves):
                by_rows(self.rows, lambda at: self.fill(self.got_down, h, at))

    def fill(self, ref, h, at):
        ref[0, h, at] = jnp.zeros((at.size, ref.shape[-1]), BF)

    def one_way(self, k, h, place, block, got, out, sems, dev):
        @pl.when(place == 0)
        def _():
            copy_to(self.parts.at[block, h], got.at[k - 1, h], sems, (k - 1, h), dev).start()

        if k < TP - 1:

            @pl.when((place >= 1) & (place + k <= TP - 1))
            def _():
                copy_to(got.at[k, h], got.at[k, h], sems, (k, h), dev).wait_recv()

                def add(at):
                    total = self.parts[block, h, at].astype(F32) + got[k, h, at].astype(F32)
                    out[k - 1, h, at] = total.astype(BF)

                by_rows(self.rows, add)
                copy_to(out.at[k - 1, h], got.at[k - 1, h], sems, (k - 1, h), dev).start()

    def step(self, k, h):
        z = self.p.z
        block = jnp.minimum(z + k, TP - 1)
        self.one_way(k, h, z, block, self.got_up, self.out_up, self.ups, self.up)
        block = jnp.maximum(z - k, 0)
        self.one_way(k, h, TP - 1 - z, block, self.got_down, self.out_down, self.downs, self.down)

    def arrive(self, h):
        z = self.p.z

        @pl.when(z >= 1)
        def _():
            got = self.got_up.at[0, h]
            copy_to(got, got, self.ups, (0, h), self.up).wait_recv()

        @pl.when(z <= TP - 2)
        def _():
            got = self.got_down.at[0, h]
            copy_to(got, got, self.downs, (0, h), self.down).wait_recv()

    def total(self, h, at):
        total = self.parts[self.p.z, h, at].astype(F32) + self.got_up[0, h, at].astype(F32)
        return total + self.got_down[0, h, at].astype(F32)

    def close(self):
        z, got = self.p.z, self.got_up.at[0, 0]
        for h in range(self.halves):
            for k in range(1, TP):

                @pl.when(z + k <= TP - 1)
                def _():
                    copy_to(got, got, self.ups, (k - 1, h), self.up).wait_send()

                @pl.when(z - k >= 0)
                def _():
                    copy_to(got, got, self.downs, (k - 1, h), self.down).wait_send()


def greet_line(p, others=()):
    barrier = pltpu.get_barrier_semaphore()
    for dev in others:
        pl.semaphore_signal(barrier, inc=1, device_id=dev, device_id_type=MESH)

    @pl.when(p.z > 0)
    def _():
        pl.semaphore_signal(barrier, inc=1, device_id=device(p, z=p.z - 1), device_id_type=MESH)

    @pl.when(p.z < TP - 1)
    def _():
        pl.semaphore_signal(barrier, inc=1, device_id=device(p, z=p.z + 1), device_id_type=MESH)

    inner = (p.z > 0) & (p.z < TP - 1)

    @pl.when(inner)
    def _():
        pl.semaphore_wait(barrier, len(others) + 2)

    @pl.when(jnp.logical_not(inner))
    def _():
        pl.semaphore_wait(barrier, len(others) + 1)


class Spread:
    KINDS = ((0, 0), (0, 1), (1, 0), (1, 1))

    def __init__(self, p, whole, sems):
        self.p, self.whole, self.started = p, whole, []
        self.xs, self.fs, self.gs, self.cs = sems[0:2], sems[2:4], sems[4:6], sems[6:8]
        self.to_x, self.to_f = device(p, x=1 - p.x), device(p, f=1 - p.f)
        self.to_c = device(p, c=1 - p.c)

    @staticmethod
    def scratch():
        return [*pairs(TP), *pairs(TP), *pairs(TP), *pairs(4, TP)]

    def slot(self, kind, d, other_core=False):
        p, (f, x) = self.p, self.KINDS[kind]
        c = 1 - p.c if other_core else p.c
        return self.whole.at[(p.f + f) % 2, 0, (p.z - d) % TP, (p.x + x) % 2, c]

    def send(self, src, dst, sems, index, dev):
        copy = copy_to(src, dst, sems, index, dev)
        copy.start()
        self.started.append(copy)

    def wait(self, ref, sems, index):
        copy_to(ref, ref, sems, index, self.to_x).wait_recv()

    def spread(self, d, src=None):
        dst = self.slot(0, d)
        src = dst if src is None else src
        self.send(src, dst, self.xs, (d,), self.to_x)
        self.send(src, dst, self.fs, (d,), self.to_f)
        self.send(src, dst, self.cs, (0, d), self.to_c)

    def given(self, d, own, by_x, by_f):
        self.send(own, self.slot(0, d), self.cs, (0, d), self.to_c)
        self.send(by_x, self.slot(1, d), self.cs, (1, d), self.to_c)
        self.send(by_f, self.slot(2, d), self.cs, (2, d), self.to_c)
        if d % 2 == 0:
            self.send(by_x, self.slot(1, d), self.gs, (d,), self.to_f)
        else:
            self.send(by_f, self.slot(2, d), self.gs, (d,), self.to_x)

    def sides(self, d):
        ref = self.slot(1, d)
        self.wait(ref, self.xs, (d,))
        if d % 2 == 0:
            self.send(ref, ref, self.gs, (d,), self.to_f)
        self.send(ref, ref, self.cs, (1, d), self.to_c)
        ref = self.slot(2, d)
        self.wait(ref, self.fs, (d,))
        if d % 2 == 1:
            self.send(ref, ref, self.gs, (d,), self.to_x)
        self.send(ref, ref, self.cs, (2, d), self.to_c)

    def corner(self, d):
        ref = self.slot(3, d)
        self.wait(ref, self.gs, (d,))
        self.send(ref, ref, self.cs, (3, d), self.to_c)

    def close(self, pieces):
        for kind in range(4):
            for d in pieces:
                self.wait(self.slot(kind, d, True), self.cs, (kind, d))
        for copy in self.started:
            copy.wait_send()


def pack_kernel(bw, gelu, lru, out_t, blocks, small, gate, up, down_t, mix, *ffw):
    p = Place()
    heads = gelu.shape[1] // bw
    part, ffw_part = -(-heads // TP) * bw, gate.shape[1] // TP
    for d in range(TP):
        z = (p.z + d) % TP
        cols = pl.ds(pl.multiple_of(z * heads // TP * bw, 128), part)
        sources = [gelu[:, cols], lru[:, cols], out_t[:, cols], blocks[...], small[...]]
        offset = 0
        for source in sources:
            mix[d, :, offset : offset + source.shape[1]] = source
            offset += source.shape[1]
        cols = pl.ds(pl.multiple_of(z * ffw_part, 128), ffw_part)
        for i, source in enumerate((gate, up, down_t)):
            ffw[d][:, i * ffw_part : (i + 1) * ffw_part] = source[:, cols]


def pack(weights, bw):
    rows, lru_width = weights[0].shape
    part = -(-lru_width // bw // TP) * bw
    mix_cols = 3 * part + weights[3].shape[1] + weights[4].shape[1]
    piece = jax.ShapeDtypeStruct((rows, 3 * weights[5].shape[1] // TP), BF)
    mix, *ffw = pl.pallas_call(
        functools.partial(pack_kernel, bw),
        in_specs=[VMEM] * 8,
        out_specs=[VMEM] * (1 + TP),
        out_shape=[jax.ShapeDtypeStruct((TP, rows, mix_cols), BF), *[piece] * TP],
        compiler_params=pltpu.CompilerParams(vmem_limit_bytes=GRANT),
    )(*weights)
    return mix, ffw


def intake_kernel(
    mix_p, ffw_0, ffw_1, x_p, cot_p, mix_w, ffw_w, piece_1, x_all, cot_all,
    zs, zr, us, ur, vs, vr, cus, cur, cvs, cvr, local, *sems
):
    p = Place()
    mix, ffw = Spread(p, mix_w, sems[:8]), Spread(p, ffw_w, sems[8:])
    to_z = [device(p, z=(p.z + d) % TP) for d in range(TP)]
    greet(to_z[1:] + [mix.to_x, mix.to_f, mix.to_c])
    started = []

    def along_z(i, src, dst, d):
        copy = copy_to(src, dst, (zs, zr), (i,), to_z[d])
        copy.start()
        started.append(copy)

    def from_z(i, ref):
        copy_to(ref, ref, (zs, zr), (i,), to_z[1]).wait_recv()

    for d in (1, 3, 2):
        along_z(d, mix_p.at[d], mix.slot(0, 0), d)
    mix.spread(0, mix_p.at[0])
    ffw.spread(0, ffw_0)
    stays = [
        pltpu.make_async_copy(mix_p.at[0], mix.slot(0, 0), local.at[0]),
        pltpu.make_async_copy(ffw_0, ffw.slot(0, 0), local.at[1]),
        pltpu.make_async_copy(x_p, x_all.at[p.z, 0], local.at[2]),
        pltpu.make_async_copy(cot_p, cot_all.at[p.z, 0], local.at[3]),
    ]
    for copy in stays:
        copy.start()
    line = Gather(p, x_all, (us, ur), (vs, vr))
    cot = Gather(p, cot_all, (cus, cur), (cvs, cvr))
    for d in (1, 3):
        from_z(d, mix.slot(0, d))
        mix.spread(d)
    line.begin(0, x_p)
    cot.begin(0, cot_p)
    from_z(2, mix.slot(0, 2))
    mix.spread(2)
    along_z(0, ffw_1, piece_1, 1)
    mix.sides(0)
    ffw.sides(0)
    mix.corner(0)
    line.step(1, 0)
    cot.step(1, 0)
    for d in (1, 3):
        mix.sides(d)
    ffw.corner(0)
    line.step(2, 0)
    cot.step(2, 0)
    for d in (1, 3):
        mix.corner(d)
    mix.sides(2)
    line.step(3, 0)
    cot.step(3, 0)
    mix.corner(2)
    from_z(0, piece_1)
    mix.close(range(TP))
    ffw.close((0,))
    for copy in started:
        copy.wait_send()
    line.close(1)
    cot.close(1)
    for copy in stays:
        copy.wait()


def intake(mix_p, ffw_0, ffw_1, x_p, cot_p, p):
    whole = lambda v: jax.ShapeDtypeStruct((p.fs, 1, TP, 2, 2) + v.shape[-2:], BF)
    mix_w, ffw_w, piece_1, x_all, cot_all = pl.pallas_call(
        intake_kernel,
        in_specs=[ANY] * 5,
        out_specs=[ANY] * 5,
        out_shape=[
            whole(mix_p),
            whole(ffw_0),
            jax.ShapeDtypeStruct(ffw_1.shape, BF),
            jax.ShapeDtypeStruct((TP, 1) + x_p.shape, BF),
            jax.ShapeDtypeStruct((TP, 1) + cot_p.shape, BF),
        ],
        scratch_shapes=[
            *pairs(TP),
            *pairs(TP - 1, 1),
            *pairs(TP - 1, 1),
            *pairs(TP - 1, 1),
            *pairs(TP - 1, 1),
            pltpu.SemaphoreType.DMA((4,)),
            *Spread.scratch(),
            *Spread.scratch(),
        ],
        compiler_params=pltpu.CompilerParams(collective_id=0, has_side_effects=True),
    )(mix_p, ffw_0, ffw_1, x_p, cot_p)
    return mix_w.reshape(-1, mix_p.shape[-1]), ffw_w, piece_1, x_all[:, 0], cot_all


class Stream:
    def __init__(self, pick, count, buffers, sems):
        self.pick, self.count, self.buffers, self.sems = pick, count, buffers, sems

    def load(self, i):
        slot = i % 2
        return pltpu.make_async_copy(self.pick(i), self.buffers.at[slot], self.sems.at[slot])

    def start(self):
        self.load(0).start()

    def run(self, low, high, body):
        def turn(i, _):
            @pl.when(i + 1 < self.count)
            def _():
                self.load(i + 1).start()

            self.load(i).wait()
            body(i, self.buffers.at[i % 2])
            return 0

        lax.fori_loop(low, high, turn, 0)


def flat(block):
    return block.reshape(-1, block.shape[-1])


FFW_CHUNK = 256


def ffw_streams(ffw_w, part, buffers):
    chunks, rest = part // FFW_CHUNK, part % FFW_CHUNK
    col = lambda base, i: pl.ds(pl.multiple_of(base + i * FFW_CHUNK, 128), FFW_CHUNK)
    pick = lambda base: lambda i: ffw_w.at[:, 0, :, :, :, :, col(base, i)]
    half = TP // 2
    rows = lambda cols: lambda i: ffw_w.at[i // 2, 0, pl.ds(i % 2 * half, half), :, :, :, cols]
    gate = Stream(pick(0), chunks, buffers[0], buffers[1])
    up = Stream(pick(part), chunks, buffers[2], buffers[3])
    down = Stream(pick(2 * part), chunks, buffers[0], buffers[1])
    down_rows = Stream(rows(pl.ds(2 * part, part)), 4, buffers[4], buffers[5])
    both_rows = Stream(rows(pl.ds(0, 2 * part)), 4, buffers[6], buffers[7])
    return gate, up, down, down_rows, both_rows


class Feed:
    def __init__(self, x, cot, ffw_w, outs, vals, scratch):
        self.x, self.cot, self.vals = x, cot, vals
        self.hidden, self.grad_pair, self.out_parts, self.in_parts = outs
        self.part = part = self.hidden.shape[1]
        self.chunks, self.rest = part // FFW_CHUNK, part % FFW_CHUNK
        streams = ffw_streams(ffw_w, part, scratch[:8])
        self.gate, self.up, self.down, self.down_rows, self.both_rows = streams
        self.tails, tail_sems = scratch[8:10]
        self.last = last = self.chunks * FFW_CHUNK
        self.loads = [
            pltpu.make_async_copy(
                ffw_w.at[:, 0, :, :, :, :, pl.ds(k * part + last, self.rest)],
                self.tails.at[k],
                tail_sems.at[k],
            )
            for k in range(3)
        ]

    def begin(self):
        self.gate.start()
        self.up.start()
        for load in self.loads:
            load.start()
        self.down_rows.start()
        self.both_rows.start()

    def cols(self, i, base):
        return pl.ds(pl.multiple_of(base + i * FFW_CHUNK, 128), FFW_CHUNK)

    def forward_cols(self, cols, other, gate_w, up_w):
        gate_vals = dot_plain(self.x[...], gate_w)
        up_vals = dot_plain(self.x[...], up_w)
        self.vals[:, cols] = gate_vals
        self.vals[:, other] = up_vals
        self.hidden[:, cols] = (gelu_pair(gate_vals)[0] * up_vals).astype(BF)

    def forward(self, low, high):
        def turn(i, _):
            for stream in (self.gate, self.up):

                @pl.when(i + 1 < self.chunks)
                def _(stream=stream):
                    stream.load(i + 1).start()

                stream.load(i).wait()
            weights = [flat(stream.buffers[i % 2]) for stream in (self.gate, self.up)]
            self.forward_cols(self.cols(i, 0), self.cols(i, self.part), *weights)
            return 0

        lax.fori_loop(low, high, turn, 0)

    def forward_end(self):
        self.down.start()
        for load in self.loads:
            load.wait()
        cols = pl.ds(self.last, self.rest), pl.ds(self.part + self.last, self.rest)
        self.forward_cols(*cols, flat(self.tails[0]), flat(self.tails[1]))

    def by_weight_rows(self, stream, source, out, low=0, high=4):
        def body(i, buffer):
            weights = flat(buffer[...])
            count = weights.shape[0]
            cols = pl.ds(pl.multiple_of(i * count, 128), count)
            out[:, cols] = dot_right_t(source[...], weights).astype(BF)

        stream.run(low, high, body)

    def forward_out(self):
        self.by_weight_rows(self.down_rows, self.hidden, self.out_parts)

    def backward_cols(self, cols, other, weights):
        grad = dot_plain(self.cot[...], weights)
        act, slope = gelu_pair(self.vals[:, cols])
        self.grad_pair[:, cols] = (grad * self.vals[:, other] * slope).astype(BF)
        self.grad_pair[:, other] = (grad * act).astype(BF)

    def backward(self, low, high):
        def body(i, buffer):
            self.backward_cols(self.cols(i, 0), self.cols(i, self.part), flat(buffer[...]))

        self.down.run(low, high, body)

    def backward_end(self):
        cols = pl.ds(self.last, self.rest), pl.ds(self.part + self.last, self.rest)
        self.backward_cols(*cols, flat(self.tails[2]))

    def backward_in(self, low, high):
        self.by_weight_rows(self.both_rows, self.grad_pair, self.in_parts, low, high)


def ffw_scratch(ffw_w, part):
    f, _, z, x, c, rows, _ = ffw_w.shape
    column = lambda width: pltpu.VMEM((2, f, z, x, c, rows, width), BF)
    wide = lambda width: pltpu.VMEM((2, z // 2, x, c, rows, width), BF)
    pair = pltpu.SemaphoreType.DMA((2,))
    return [
        column(FFW_CHUNK), pair, column(FFW_CHUNK), pair, wide(part), pair, wide(2 * part), pair,
        pltpu.VMEM((3, f, z, x, c, rows, part % FFW_CHUNK), BF),
        pltpu.SemaphoreType.DMA((3,)),
    ]


def middle_kernel(with_ffw, *refs):
    parts, x_zero, gain, cot_p, cot_first, piece_1, by_x, by_f, piece_2, piece_3, _ = refs[:11]
    x_one_out, ffw_out, cot_out, ffw_w, *refs = refs[11:]
    if with_ffw:
        hidden_out, pair_out, parts_out, in_out, *refs = refs
    x_one, ffw_all, cot_all, own, local, gu0, gu1, gd0, gd1, cu0, cu1, cd0, cd1 = refs[:13]
    p = Place()
    line = LineSum(p, parts, refs[13:21])
    out = Gather(p, ffw_all, (gu0, gu1), (gd0, gd1))
    cot = Gather(p, cot_all, (cu0, cu1), (cd0, cd1))
    halves, rows = parts.shape[1:3]
    line.clear()
    stays = []

    def stay(src, dst):
        copy = pltpu.make_async_copy(src, dst, local.at[len(stays)])
        copy.start()
        stays.append(copy)

    if with_ffw:
        ffw = Spread(p, ffw_w, refs[21:29])
        outs, vals, buffers = refs[29:33], refs[33], refs[34:44]
        bounce_sems = refs[44]
        greet_line(p, (ffw.to_x, ffw.to_f, ffw.to_c))
    else:
        greet_line(p)
    side = lambda name, *args: getattr(ffw, name)(*args) if with_ffw else None
    for h in range(halves):
        line.step(TP - 1, h)
    stay(cot_first, cot_all.at[:, pl.ds(0, 1)])
    side("given", 1, piece_1, by_x, by_f)
    side("spread", 3, piece_3)
    side("spread", 2, piece_2)
    if with_ffw:
        part = vals.shape[1] // 2
        moves = [(piece_1, 0, 1), (by_x, 1, 1), (by_f, 2, 1), (piece_3, 0, 3), (piece_2, 0, 2)]
        steps = [(src, ffw.slot(kind, d), k) for src, kind, d in moves for k in range(2)]

        def bounce(i, out):
            src, dst, k = steps[i]
            cols = pl.ds(0, 2 * part) if k == 0 else pl.ds(2 * part, part)
            space = buffers[6 - 2 * k].at[i // 2 % 2, 0, 0, 0]
            if out:
                return pltpu.make_async_copy(space, dst.at[:, cols], bounce_sems.at[i % 4])
            return pltpu.make_async_copy(src.at[:, cols], space, bounce_sems.at[4])

        for i in range(len(steps)):
            if i >= 4:
                bounce(i - 4, True).wait()
            bounce(i, False).start()
            bounce(i, False).wait()
            bounce(i, True).start()
        for i in range(len(steps) - 4, len(steps)):
            bounce(i, True).wait()
    for k in range(TP - 2, 0, -1):
        for h in range(halves):
            line.step(k, h)
    for h in range(halves):
        line.arrive(h)

        def finish(at, h=h):
            value = x_zero[h, at].astype(F32) + line.total(h, at)
            x_one[h, at] = value
            own[h, at] = normed(value, gain[...]).astype(BF)

        by_rows(rows, finish)
        out.begin(h, own.at[h])
        stay(own.at[h], ffw_all.at[p.z, h])
    for h in range(halves):
        out.step(1, h)
    for d in (3, 2):
        side("sides", d)
    for h in range(halves):
        out.step(2, h)
    cot.begin(1, cot_p)
    stay(cot_p, cot_all.at[p.z, 1])
    side("corner", 1)
    for d in (3, 2):
        side("corner", d)
    for h in range(halves):
        out.step(3, h)
    cot.step(1, 1)
    side("close", (1, 2, 3))
    if not with_ffw:
        cot.step(2, 1)
        cot.step(3, 1)
    for copy in stays:
        copy.wait()
    done = len(stays)
    stay(x_one, x_one_out)
    stay(ffw_all, ffw_out)
    if not with_ffw:
        stay(cot_all, cot_out)
    else:
        tokens = lambda ref: ref.reshape(TP * halves * rows, parts.shape[3])
        hidden, pair, out_parts, in_parts = outs
        flat_outs = (hidden, pair, tokens(out_parts), in_parts)
        feed = Feed(tokens(ffw_all), tokens(cot_all), ffw_w, flat_outs, vals, buffers)
        feed.begin()
        feed.forward(0, 2)
        cot.step(2, 1)
        feed.forward(2, 6)
        cot.step(3, 1)
        stay(cot_all, cot_out)
        feed.forward(6, feed.chunks)
        feed.forward_end()
        feed.forward_out()
        stay(hidden, hidden_out)
        stay(out_parts, parts_out)
        feed.backward(0, feed.chunks)
        feed.backward_end()
        stay(pair, pair_out)
        feed.backward_in(0, 4)
        stay(in_parts, in_out)
    line.close()
    out.close(halves)
    cot.close((1,))
    for copy in stays[done:]:
        copy.wait()


def middle(parts, x_zero, gain, cot_p, cot_first, pieces, ffw_w):
    shape = parts.shape
    with_ffw = ffw_w is not None
    line = (TP, 2) + cot_p.shape
    outs, extra = [], []
    if with_ffw:
        tokens, part = shape[0] * shape[1] * shape[2], ffw_w.shape[-1] // 3
        assert part // FFW_CHUNK >= 6 and part % FFW_CHUNK
        outs = [(tokens, part), (tokens, 2 * part), shape, (tokens, shape[3])]
        extra = [
            *Spread.scratch(),
            *(pltpu.VMEM(kept, BF) for kept in outs),
            pltpu.VMEM((tokens, 2 * part), F32),
            *ffw_scratch(ffw_w, part),
            pltpu.SemaphoreType.DMA((5,)),
        ]
    else:
        ffw_w = jnp.zeros((16, 128), BF)
        pieces = [ffw_w] * 5
    return pl.pallas_call(
        functools.partial(middle_kernel, with_ffw),
        in_specs=[VMEM] * 3 + [ANY] * 8,
        out_specs=[ANY] * (4 + len(outs)),
        out_shape=[
            jax.ShapeDtypeStruct(shape[1:], F32),
            jax.ShapeDtypeStruct(shape, BF),
            jax.ShapeDtypeStruct(line, BF),
            jax.ShapeDtypeStruct(ffw_w.shape, BF),
            *(jax.ShapeDtypeStruct(out, BF) for out in outs),
        ],
        input_output_aliases={10: 3},
        scratch_shapes=[
            pltpu.VMEM(shape[1:], F32),
            pltpu.VMEM(shape, BF),
            pltpu.VMEM(line, BF),
            pltpu.VMEM(shape[1:], BF),
            pltpu.SemaphoreType.DMA((shape[1] + 10,)),
            *pairs(TP - 1, shape[1]),
            *pairs(TP - 1, shape[1]),
            *pairs(TP - 1, 2),
            *pairs(TP - 1, 2),
            *LineSum.scratch(shape),
            *extra,
        ],
        compiler_params=pltpu.CompilerParams(
            collective_id=1, has_side_effects=True, vmem_limit_bytes=GRANT
        ),
    )(parts, x_zero, gain, cot_p, cot_first, *pieces, ffw_w)


def norm_back(values, gain, grad):
    inv = lax.rsqrt(jnp.mean(values * values, axis=-1, keepdims=True) + EPS)
    unit = values * inv
    through = grad * gain
    inner = jnp.mean(through * unit, axis=-1, keepdims=True)
    return inv * (through - unit * inner), grad * unit


class Fold:
    ORDER = ((0, 1, 1), (1, 1, 1), (0, 0, 1), (1, 1, 0), (0, 1, 0), (1, 0, 1), (0, 0, 0), (1, 0, 0))

    def __init__(self, p, grad, cores, scratch):
        self.p, self.grad, self.cores = p, grad, cores
        self.sums, self.stage, self.got, self.got_late = scratch[:4]
        self.near, self.staged = scratch[4:6]
        self.core_sems, self.early, self.late = scratch[6:8], scratch[8:10], scratch[10:12]
        self.to = (device(p, x=1 - p.x), device(p, f=1 - p.f))
        self.to_c = device(p, c=1 - p.c)

    @staticmethod
    def shapes(grad, staged):
        block = (TP // 2,) + grad.shape[-2:]
        waiting = (2,) if staged else (2, 2, 2)
        return jax.ShapeDtypeStruct((2, 2, 2) + block, BF), [
            pltpu.VMEM((2, 2, 2) + block, BF),
            pltpu.VMEM(waiting + block, BF),
            pltpu.VMEM((2, 2) + block, BF),
            pltpu.VMEM((2,) + block, BF),
            pltpu.SemaphoreType.DMA((8,)),
            pltpu.SemaphoreType.DMA((2,)),
            *pairs(8),
            *pairs(2, 2),
            *pairs(2),
        ]

    def block(self, way, f_rel, x_rel, c):
        p, half = self.p, TP // 2
        f, x = (p.f + f_rel) % 2, (p.x + x_rel) % 2
        return self.grad.at[f, 0, pl.ds(way * half, half), x, c]

    def cross(self, i):
        name = self.ORDER[i]
        src = self.block(*name, 1 - self.p.c)
        dst = self.stage if self.cores is None else self.cores
        return copy_to(src, dst.at[name], self.core_sems, (i,), self.to_c)

    def load(self, i):
        name = self.ORDER[i]
        return pltpu.make_async_copy(
            self.block(*name, self.p.c), self.sums.at[name], self.near.at[i]
        )

    def fetch(self, i):
        src = self.cores.at[self.ORDER[i]]
        return pltpu.make_async_copy(src, self.stage.at[i % 2], self.staged.at[i % 2])

    def first(self, way, block):
        src = self.sums.at[(0, block, 1) if way == 0 else (1, 1, block)]
        return copy_to(src, self.got.at[way, block], self.early, (way, block), self.to[way])

    def second(self, way):
        src = self.sums.at[(0, 1, 0) if way == 0 else (1, 0, 1)]
        return copy_to(src, self.got_late.at[way], self.late, (way,), self.to[1 - way])

    def add(self, name, *others):
        rows = self.sums.shape[-2]

        def turn(at):
            for k in range(TP // 2):
                total = self.sums[(*name, k, at)].astype(F32)
                for other in others:
                    total = total + other[k, at].astype(F32)
                self.sums[(*name, k, at)] = total.astype(BF)

        by_rows(rows, turn)

    def begin(self, blocks=range(8)):
        for i in blocks:
            self.cross(i).start()
            self.load(i).start()

    def issue(self, i):
        self.cross(i).wait_recv()
        self.fetch(i).start()

    def join(self, i):
        if self.cores is None:
            self.cross(i).wait_recv()
            self.load(i).wait()
            self.add(self.ORDER[i], self.stage.at[self.ORDER[i]])
        else:
            if i == 0:
                self.issue(0)
            if i + 1 < 8:
                self.issue(i + 1)
            self.fetch(i).wait()
            self.load(i).wait()
            self.add(self.ORDER[i], self.stage.at[i % 2])
        if i < 4:
            way = self.ORDER[i][0]
            self.first(way, self.ORDER[i][1 + way]).start()

    def middle(self):
        for way in range(2):
            self.first(way, 1).wait_recv()
            self.add((0, 1, 0) if way == 0 else (1, 0, 1), self.got.at[way, 1])
            self.second(way).start()

    def finish(self):
        for way in range(2):
            self.first(way, 0).wait_recv()
            self.second(way).wait_recv()
            self.add((way, 0, 0), self.got.at[way, 0], self.got_late.at[way])

    def result(self, z):
        return self.sums.at[z // (TP // 2), 0, 0, z % (TP // 2)]

    def close(self):
        for i in range(8):
            self.cross(i).wait_send()
        for way in range(2):
            self.second(way).wait_send()
            for block in range(2):
                self.first(way, block).wait_send()


def folds_of(p, grads, cores, scratch):
    return [Fold(p, g, c, scratch[12 * i : 12 * i + 12]) for i, (g, c) in enumerate(zip(grads, cores))]


GRAD_CHUNK = 640


class Outer:
    def __init__(self, grad, left, right, turned, buffers, sems):
        self.grad, self.left, self.right, self.turned = grad, left, right, turned
        self.buffers, self.sems = buffers, sems
        self.wide = buffers.shape[-1]
        self.across = grad.shape[-1] // self.wide
        self.count = 4 * self.across

    def place(self, i):
        return (lax.axis_index("fsdp") * 2 + 2 + i // self.across) % 4

    def store(self, i):
        k, half = self.place(i), TP // 2
        cols = pl.ds(pl.multiple_of(i % self.across * self.wide, 128), self.wide)
        dst = self.grad.at[k // 2, 0, pl.ds(k % 2 * half, half), :, :, :, cols]
        return pltpu.make_async_copy(self.buffers.at[i % 2], dst, self.sems.at[i % 2])

    def run(self, low, high):
        rows = self.turned.shape[0]

        def turn(i, _):
            @pl.when(i % self.across == 0)
            def _():
                cols = pl.ds(pl.multiple_of(self.place(i) * rows, 128), rows)
                self.turned[...] = jnp.transpose(self.left[:, cols])

            @pl.when(i >= low + 2)
            def _():
                self.store(i - 2).wait()

            cols = pl.ds(pl.multiple_of(i % self.across * self.wide, 128), self.wide)
            chunk = dot_plain(self.turned[...], self.right[:, cols]).astype(BF)
            self.buffers[i % 2] = chunk.reshape(self.buffers.shape[1:])
            self.store(i).start()
            return 0

        lax.fori_loop(low, high, turn, 0)

    def flush(self, done):
        for i in (done - 2, done - 1):
            self.store(i).wait()


def turn_kernel(count, *refs):
    parts, out_parts, x_one, cot, gain = refs[:5]
    factors, refs = refs[5 : 5 + (4 if count else 0)], refs[5 + (4 if count else 0) :]
    mixed_out, grad_x_one, grad_gain, mix_all = refs[:4]
    pieces, refs = refs[4 : 4 + TP], refs[4 + TP :]
    grads, cores, refs = refs[:count], refs[count : 2 * count], refs[2 * count :]
    own, local, gu0, gu1, gd0, gd1 = refs[:6]
    p = Place()
    line, late = LineSum(p, parts, refs[6:14]), LineSum(p, out_parts, refs[14:22])
    folds = folds_of(p, grads, cores, refs[22 : 22 + 12 * count])
    out = Gather(p, mix_all, (gu0, gu1), (gd0, gd1))
    halves, rows = parts.shape[1:3]
    line.clear()
    late.clear()
    greet_line(p, (*folds[0].to, folds[0].to_c) if folds else ())
    stays = []

    def stay(src, dst):
        copy = pltpu.make_async_copy(src, dst, local.at[len(stays)])
        copy.start()
        stays.append(copy)

    if folds:
        left, right, turned, buffers, chunk_sems, load_sems = refs[22 + 12 * count :]
        part = factors[1].shape[1]
        outers = [
            Outer(grads[m], left, right.at[:, pl.ds(m // 2 * part, part)], turned, buffers, chunk_sems)
            for m in range(3)
        ]
        down, gate, up = folds
        size = outers[0].count
        half = size // 2

    def load(m):
        cols = right.at[:, pl.ds(0, factors[2 * m + 1].shape[1])]
        copies = [
            pltpu.make_async_copy(factors[2 * m], left, load_sems.at[0]),
            pltpu.make_async_copy(factors[2 * m + 1], cols, load_sems.at[1]),
        ]
        for copy in copies:
            copy.start()
        for copy in copies:
            copy.wait()

    def outer(m, low, high):
        outers[m].run(low, high)
        outers[m].flush(high)
        folds[m].begin((0, 1, 3, 4) if high == half else (2, 5, 6, 7))

    def join(fold, *blocks):
        for i in blocks:
            fold.join(i)

    def line_step(k):
        for h in range(halves):
            line.step(k, h)

    line_step(3)
    for h in range(halves):
        late.step(TP - 1, h)
    if folds:
        load(0)
        outer(0, 0, half)
        outer(0, half, size)
        join(down, 0, 1)
        load(1)
        outer(1, 0, half)
        join(down, 2, 3)
    line_step(2)
    if folds:
        outer(1, half, size)
        join(down, 4, 5)
        outer(2, 0, half)
        join(gate, 0, 1)
        down.middle()
        join(gate, 2, 3)
    line_step(1)
    if folds:
        outer(2, half, size)
        join(gate, 4, 5)
    grad_gain[...] = jnp.zeros(grad_gain.shape, F32)
    for h in range(halves):
        line.arrive(h)

        def finish(at, h=h):
            grad, gains = norm_back(x_one[h, at], gain[...], line.total(h, at))
            grad = grad + cot[h, at].astype(F32)
            grad_x_one[h, at] = grad
            own[h, at] = grad.astype(BF)
            grad_gain[0:1] += jnp.sum(gains, axis=0, keepdims=True)

        by_rows(rows, finish)
        out.begin(h, own.at[h])
        stay(own.at[h], mix_all.at[p.z, h])
    if folds:
        join(up, 0, 1)
        gate.middle()
        join(up, 2, 3)
    for h in range(halves):
        out.step(1, h)
        late.step(2, h)
    if folds:
        join(down, 6, 7)
        join(up, 4, 5)
        join(gate, 6, 7)
    for h in range(halves):
        out.step(2, h)
        late.step(1, h)
    if folds:
        join(up, 6, 7)
        up.middle()
    for h in range(halves):
        out.step(3, h)
    for h in range(halves):
        late.arrive(h)

        def store(at, h=h):
            mixed_out[h, at] = (x_one[h, at] + late.total(h, at)).astype(BF)

        by_rows(rows, store)
    offset = 0
    for fold in folds:
        fold.finish()
        cols = fold.grad.shape[-1]
        for d in range(TP):
            stay(fold.result((p.z + d) % TP), pieces[d].at[:, pl.ds(offset, cols)])
        offset += cols
    for fold in folds:
        fold.close()
    line.close()
    late.close()
    out.close(halves)
    for copy in stays:
        copy.wait()


def turn(parts, out_parts, x_one, cot, gain, factors, p):
    shape, count, width = parts.shape, 3 if factors else 0, parts.shape[-1]
    rows = width // (p.fs * TP * 4)
    sizes = [factors[1].shape[1]] * count if factors else []
    grads = [jax.ShapeDtypeStruct((p.fs, 1, TP, 2, 2, rows, size), BF) for size in sizes]
    folded = [Fold.shapes(grad, True) for grad in grads]
    piece = jax.ShapeDtypeStruct((rows, sum(sizes)) if factors else (16, 128), BF)
    extra = []
    if factors:
        assert all(size % GRAD_CHUNK == 0 for size in sizes)
        tokens, deep = factors[0].shape[0], width // 4
        extra = [
            pltpu.VMEM((tokens, width), BF),
            pltpu.VMEM((tokens, 2 * sizes[0]), BF),
            pltpu.VMEM((deep, tokens), BF),
            pltpu.VMEM((2, TP // 2, 2, 2, rows, GRAD_CHUNK), BF),
            pltpu.SemaphoreType.DMA((2,)),
            pltpu.SemaphoreType.DMA((2,)),
        ]
    results = pl.pallas_call(
        functools.partial(turn_kernel, count),
        in_specs=[VMEM] * 5 + [ANY] * len(factors),
        out_specs=[VMEM, VMEM, VMEM, ANY] + [ANY] * (TP + 2 * count),
        out_shape=[
            jax.ShapeDtypeStruct(shape[1:], BF),
            jax.ShapeDtypeStruct(shape[1:], F32),
            jax.ShapeDtypeStruct((8, width), F32),
            jax.ShapeDtypeStruct(shape, BF),
            *[piece] * TP,
            *grads,
            *(cores for cores, _ in folded),
        ],
        scratch_shapes=[
            pltpu.VMEM(shape[1:], BF),
            pltpu.SemaphoreType.DMA((shape[1] + TP * count,)),
            *pairs(TP - 1, shape[1]),
            *pairs(TP - 1, shape[1]),
            *LineSum.scratch(shape),
            *LineSum.scratch(shape),
            *(item for _, scratch in folded for item in scratch),
            *extra,
        ],
        compiler_params=pltpu.CompilerParams(
            collective_id=2, has_side_effects=True, vmem_limit_bytes=GRANT
        ),
    )(parts, out_parts, x_one, cot, gain, *factors)
    return results[: 4 + TP]


def final_kernel(*refs):
    parts, x_zero, gain, grad_x_one, vectors, blocks = refs[:6]
    factors, refs = refs[6:10], refs[10:]
    grad_in, sums = refs[:2]
    outs, grads, refs = refs[2:6], (blocks, *refs[6:9]), refs[9:]
    acc, got, vs, vr, zs, zr, local, left, right, turned, buffers, chunk_sems, load_sems = refs[:13]
    p = Place()
    line = LineSum(p, parts, refs[13:21])
    folds = folds_of(p, grads, [None] * 4, refs[21:])
    halves, rows = parts.shape[1:3]
    line.clear()
    to_z = [device(p, z=(p.z + d) % TP) for d in range(TP)]
    (to_x, to_f), to_c = folds[0].to, folds[0].to_c
    greet(to_z[1:] + [to_x, to_f, to_c])
    partners = [to_c, to_x, to_f] + [
        device(p, z=p.z + bit * (1 - 2 * (p.z // bit % 2))) for bit in (1, 2)
    ]
    part = factors[1].shape[1]
    outers = [
        Outer(grads[m], left, right.at[:, pl.ds(m // 3 * part, part)], turned, buffers, chunk_sems)
        for m in range(1, 4)
    ]

    def load(m):
        cols = right.at[:, pl.ds(0, factors[2 * m + 1].shape[1])]
        copies = [
            pltpu.make_async_copy(factors[2 * m], left, load_sems.at[0]),
            pltpu.make_async_copy(factors[2 * m + 1], cols, load_sems.at[1]),
        ]
        for copy in copies:
            copy.start()
        for copy in copies:
            copy.wait()

    def outer(m):
        outers[m - 1].run(0, outers[m - 1].count)
        outers[m - 1].flush(outers[m - 1].count)
        folds[m].begin()

    def join(m, *blocks):
        for i in blocks:
            folds[m].join(i)

    def line_step(k):
        for h in range(halves):
            line.step(k, h)

    def vector(i):
        return copy_to(acc.at[i], got.at[i], (vs, vr), (i,), partners[i])

    def next_vector(i):
        vector(i).wait_recv()
        if i < 4:
            acc[i + 1] = acc[i] + got[i]
            vector(i + 1).start()
        else:
            sums[...] = acc[i] + got[i]

    started, stays = [], []

    def send_on(m):
        folds[m].finish()
        for d in (1, 3, 2):
            src = folds[m].result((p.z + d) % TP)
            copy = copy_to(src, outs[m].at[p.z], (zs, zr), (m, d - 1), to_z[d])
            copy.start()
            started.append(copy)
        stays.append(pltpu.make_async_copy(folds[m].result(p.z), outs[m].at[p.z], local.at[m]))
        stays[-1].start()

    acc[0] = vectors[...]
    vector(0).start()
    folds[0].begin()
    line_step(3)
    load(0)
    outer(1)
    load(1)
    join(0, 0, 1, 2, 3)
    outer(2)
    join(0, 4, 5)
    join(1, 0, 1)
    folds[0].middle()
    join(1, 2, 3)
    outer(3)
    line_step(2)
    next_vector(0)
    for m in (1, 2):
        join(m - 1, 6, 7)
        join(m, 4, 5)
        join(m + 1, 0, 1)
        folds[m].middle()
        join(m + 1, 2, 3)
        if m == 1:
            line_step(1)
        next_vector(m)
        send_on(m - 1)
    join(2, 6, 7)
    join(3, 4, 5)
    folds[3].middle()
    join(3, 6, 7)
    send_on(2)
    next_vector(3)
    for h in range(halves):
        line.arrive(h)

        def finish(at, h=h):
            grad, _ = norm_back(x_zero[h, at].astype(F32), gain[...], line.total(h, at))
            grad_in[h, at] = grad_x_one[h, at] + grad

        by_rows(rows, finish)
    next_vector(4)
    send_on(3)
    for m in range(4):
        for d in range(1, TP):
            ref = outs[m].at[(p.z - d) % TP]
            copy_to(ref, ref, (zs, zr), (m, d - 1), to_z[1]).wait_recv()
    for copy in started:
        copy.wait_send()
    for i in range(5):
        vector(i).wait_send()
    for fold in folds:
        fold.close()
    line.close()
    for copy in stays:
        copy.wait()


def final(parts, x_zero, gain, grad_x_one, vectors, blocks, factors, p):
    shape = parts.shape
    rows, part = blocks.shape[-2], factors[1].shape[1]
    tokens, width = factors[0].shape
    shaped = jax.ShapeDtypeStruct
    grads = [shaped((p.fs, 1, TP, 2, 2, rows, part), BF)] * 3
    widths = [blocks.shape[-1]] + [part] * 3
    folded = [Fold.shapes(grad, False)[1] for grad in (blocks, *grads)]
    results = pl.pallas_call(
        final_kernel,
        in_specs=[VMEM] * 5 + [ANY] * 5,
        out_specs=[VMEM, VMEM] + [ANY] * 7,
        out_shape=[
            shaped(shape[1:], F32),
            shaped(vectors.shape, F32),
            *(shaped((TP, rows, wide), BF) for wide in widths),
            *grads,
        ],
        scratch_shapes=[
            pltpu.VMEM((5,) + vectors.shape, F32),
            pltpu.VMEM((5,) + vectors.shape, F32),
            *pairs(5),
            *pairs(4, TP - 1),
            pltpu.SemaphoreType.DMA((4,)),
            pltpu.VMEM((tokens, width), BF),
            pltpu.VMEM((tokens, 2 * part), BF),
            pltpu.VMEM((width // 4, tokens), BF),
            pltpu.VMEM((2, TP // 2, 2, 2, rows, part), BF),
            pltpu.SemaphoreType.DMA((2,)),
            pltpu.SemaphoreType.DMA((2,)),
            *LineSum.scratch(shape),
            *(item for scratch in folded for item in scratch),
        ],
        compiler_params=pltpu.CompilerParams(
            collective_id=3, has_side_effects=True, vmem_limit_bytes=GRANT
        ),
    )(parts, x_zero, gain, grad_x_one, vectors, blocks, *factors)
    return results[0], results[1], results[2:6]


def chain_kernel(backward, sums, *refs):
    if backward:
        known, start, spans, send, recv = refs
    else:
        start, spans, send, recv = refs
    p = Place()
    peers = [device_q(p, (p.q + d) % NQ) for d in range(NQ)]
    greet(peers[1:])
    spans[p.q] = sums[...]
    copies = []
    for d in range(1, NQ):
        copies.append(copy_to(spans.at[p.q], spans.at[p.q], (send, recv), (d,), peers[d]))
        copies[-1].start()
    for d in range(1, NQ):
        ref = spans.at[(p.q - d) % NQ]
        copy_to(ref, ref, (send, recv), (d,), peers[d]).wait_recv()
    micro = sums.shape[1] // TP
    carry = jnp.zeros((micro, sums.shape[2]), F32)
    order = [(z, q) for z in range(TP) for q in range(NQ)]
    for z, q in reversed(order) if backward else order:
        here = slice(z * micro, (z + 1) * micro)

        @pl.when(p.q == q)
        def _(carry=carry, here=here):
            start[here] = carry

        decay = known[q, 0, here] if backward else spans[q, 0, here]
        carry = decay * carry + spans[q, 0 if backward else 1, here]
    for copy in copies:
        copy.wait_send()


def device_q(p, q):
    return device(p, x=q // 2, c=q % 2)


def chain(sums, known=None):
    backward = known is not None
    every = (NQ,) + sums.shape
    return pl.pallas_call(
        functools.partial(chain_kernel, backward),
        in_specs=[VMEM] * (2 if backward else 1),
        out_specs=[VMEM, VMEM],
        out_shape=[
            jax.ShapeDtypeStruct(sums.shape[1:], F32),
            jax.ShapeDtypeStruct(every, F32),
        ],
        scratch_shapes=pairs(NQ),
        cost_estimate=FREE,
        compiler_params=pltpu.CompilerParams(
            collective_id=5 if backward else 4, has_side_effects=True
        ),
    )(*((sums, known) if backward else (sums,)))


def unpack_kernel(own, one, two, three, *outs):
    p = Place()
    part = own.shape[1] // len(outs)
    for d, piece in enumerate((own, one, two, three)):
        cols = pl.ds(pl.multiple_of((p.z - d) % TP * part, 128), part)
        for i, out in enumerate(outs):
            out[:, cols] = piece[:, i * part : (i + 1) * part].astype(F32)


def unpack(pieces, count):
    rows, cols = pieces[0].shape
    return pl.pallas_call(
        unpack_kernel,
        in_specs=[VMEM] * TP,
        out_specs=[VMEM] * count,
        out_shape=[jax.ShapeDtypeStruct((rows, cols // count * TP), F32)] * count,
        compiler_params=pltpu.CompilerParams(vmem_limit_bytes=GRANT),
    )(*pieces)


def geglu(gate_vals, up_vals):
    return jax.nn.gelu(gate_vals) * up_vals


def all_spans(value, p):
    by_q = everywhere(value, shift_q, p.q, NQ)
    by_r = everywhere(by_q, shift_r, p.r, p.rests)
    return jnp.swapaxes(by_r, 1, 2).reshape((-1,) + value.shape[1:])


def own_spans(spans, p):
    split = spans.reshape((p.rests, TP, NQ) + spans.shape[1:])
    return lax.dynamic_index_in_dim(at(split, p.r), p.q, 1, keepdims=False)


def on_device(
    inputs,
    cotangent,
    proj_gelu,
    proj_lru,
    gate_blocks,
    proj_out,
    ffw_gate,
    ffw_up,
    ffw_down,
    norm_mix,
    norm_ffw,
    decay_param,
    conv_taps,
):
    p = Place()
    micro, span, width = inputs.shape[0], inputs.shape[2], inputs.shape[3]
    lru_width = proj_gelu.shape[1]
    tap_count = conv_taps.shape[1]
    block_width = gate_blocks.shape[1] // 2
    heads = lru_width // block_width
    ffw_part = ffw_gate.shape[1] // TP
    rows = proj_gelu.shape[0]
    held = -(-heads // TP)
    first = [k * heads // TP for k in range(TP)]
    owned = [range(first[k], first[k + 1] if k + 1 < TP else heads) for k in range(TP)]
    part = held * block_width

    out_t, down_t = proj_out.T, ffw_down.T
    small = jnp.concatenate([norm_mix[None], norm_ffw[None], decay_param[None], conv_taps.T])
    small = jnp.pad(small, ((0, 128 - small.shape[0]), (0, 0))).T
    x_rows, cot = inputs[:, 0], cotangent[:, 0]
    one = 1 if p.rests == 1 else 0
    cot_halves = cot.reshape(2, -1, width)
    edge = lax.ppermute(
        x_rows[:, span - (tap_count - 1) :],
        "seq",
        [(i, i + 1) for i in range(lax.axis_size("seq") - 1)],
    )
    edge = jnp.pad(edge, ((0, 0), (HALO - (tap_count - 1), 0), (0, 0)))
    x_wide = jnp.concatenate([x_rows.reshape(-1, width), edge.reshape(-1, width)])
    if p.rests == 1:
        weights = (proj_gelu, proj_lru, out_t, gate_blocks, small, ffw_gate, ffw_up, down_t)
        mix_pieces, ffw_pieces = pack(weights, block_width)
        mix_w, ffw_w, piece_1, x_all, cot_first = intake(
            mix_pieces, ffw_pieces[0], ffw_pieces[1], x_wide, cot_halves[0], p
        )
        piece_2, piece_3, x_all = lax.optimization_barrier((*ffw_pieces[2:], x_all))
        piece_3, piece_2 = shift_z(piece_3, 3), shift_z(piece_2, 2)
        passed = (piece_1, swap_x(piece_1), swap_f(piece_1), piece_2, piece_3)
    else:
        mix_pieces, ffw_pieces = [], []
        for k in range(TP):
            cols = slice(first[k] * block_width, first[k] * block_width + part)
            pieces = [proj_gelu[:, cols], proj_lru[:, cols], out_t[:, cols], gate_blocks, small]
            mix_pieces.append(jnp.concatenate(pieces, axis=1))
            cols = slice(k * ffw_part, (k + 1) * ffw_part)
            pieces = [ffw_gate[:, cols], ffw_up[:, cols], down_t[:, cols]]
            ffw_pieces.append(jnp.concatenate(pieces, axis=1))
        mix_w = weights_in(jnp.stack(mix_pieces), p)
        whole_ffw = weights_in(jnp.stack(ffw_pieces), p)
        x_all, passed, ffw_w = gather_z(x_wide, p), None, None
        cot_first = gather_z(cot_halves[:1], p)
    dims = (span, micro, heads, held, block_width, tap_count)
    small_w, rows_w, mixed, pre, conv, gate, state, prod, sums = recur(
        x_all.reshape(-1, width), mix_w, dims
    )
    mix_gain, ffw_gain = small_w[0:1], small_w[1:2]
    start = sum(jnp.where(p.z == k, first[k] * block_width, 0) for k in range(TP))

    ends = (TP, micro, part)
    if p.rests == 1:
        state_in, every_sum = chain(sums)
    else:
        sums = all_spans(jnp.stack([sums[0].reshape(ends), sums[1].reshape(ends)], axis=1), p)
        carry, carries = jnp.zeros_like(sums[0, 0]), []
        for k in range(sums.shape[0]):
            carries.append(carry)
            carry = sums[k, 0] * carry + sums[k, 1]
        state_in = own_spans(jnp.stack(carries), p).reshape(-1, part)
    mix_bf, out_parts = recur_mix(pre, rows_w, state, prod, state_in, mix_w, dims)
    blocked = (TP, micro * CUTS, span // CUTS, width)
    x_own, cot_own = x_rows.reshape(blocked[1:]), cot.reshape(blocked[1:])
    out_parts = out_parts.reshape(blocked)
    x_one, ffw_bf, cot_all, _, *fed = middle(
        out_parts, x_own, ffw_gain, cot_halves[1], cot_first, passed, ffw_w
    )
    cot_all = cot_all.reshape(-1, width)

    ffw_bf = ffw_bf.reshape(-1, width)
    if p.rests == 1:
        hidden_bf, grad_gate_up, ffw_parts, grad_in_parts = fed
    else:
        gate_up_w, down_w = whole_ffw[:, : 2 * ffw_part], whole_ffw[:, 2 * ffw_part :]
        gate_up = dot_plain(ffw_bf, gate_up_w)
        gate_vals, up_vals = gate_up[:, :ffw_part], gate_up[:, ffw_part:]
        hidden_bf = geglu(gate_vals, up_vals).astype(BF)
        grad_hidden = dot_plain(cot_all, down_w)
        _, pull_back = jax.vjp(geglu, gate_vals, up_vals)
        grad_gate_up = jnp.concatenate(pull_back(grad_hidden), axis=1).astype(BF)
        ffw_parts = dot_right_t(hidden_bf, down_w).astype(BF)
        grad_in_parts = dot_right_t(grad_gate_up, gate_up_w).astype(BF)
    ffw_parts, grad_in_parts = ffw_parts.reshape(blocked), grad_in_parts.reshape(blocked)
    factors = [cot_all, hidden_bf, ffw_bf, grad_gate_up]
    mixed_out, grad_x_one, gain_rows, grad_mix, *ffw_pieces = turn(
        grad_in_parts, ffw_parts, x_one, cot_own, ffw_gain, factors * one, p
    )
    if p.rests == 1:
        for d in (1, 3, 2):
            ffw_pieces[d] = shift_z(ffw_pieces[d], d)
    grad_mix = grad_mix.reshape(-1, width)

    grad_gelu_bf, local_back, prod_back, back_sums = recur_back(
        grad_mix, pre, rows_w, state, prod, state_in, gate, mix_w, dims
    )
    if p.rests == 1:
        carried, _ = chain(back_sums[None], every_sum)
    else:
        back_sums = all_spans(back_sums.reshape(ends), p)
        carry, carries = jnp.zeros_like(sums[0, 0]), []
        for k in range(sums.shape[0] - 1, -1, -1):
            carries.append(carry)
            carry = sums[k, 0] * carry + back_sums[k]
        carried = own_spans(jnp.stack(carries[::-1]), p).reshape(-1, part)
    block_mats = lax.dynamic_slice(mix_w, (start, 3 * part), (part, 2 * block_width))
    grad_blocks, grad_lru, spill, row_grads = recur_grad(
        local_back, prod_back, carried, state, prod, state_in, gate, conv, pre, rows_w,
        block_mats.reshape(held, block_width, 2 * block_width), dims,
    )
    spill = spill.reshape(TP, micro, HALO, part)
    from_next = shift_q(spill, -1)
    last = jnp.zeros_like(spill[:1])
    if p.rests > 1:
        last = move(spill[:1], lambda r, z, q: (r - 1, z, NQ - 1) if q == 0 and r > 0 else None)
    from_next = jnp.where(
        p.q == NQ - 1, jnp.concatenate([from_next[1:], last], axis=0), from_next
    )
    grad_pair, grad_mixed_parts, mix_gain_rows = recur_in(
        grad_gelu_bf, grad_lru, from_next.reshape(-1, part), rows_w, small_w, mixed, mix_w, dims
    )
    grad_mixed_parts = grad_mixed_parts.reshape(blocked)

    blocks_all = lax.dynamic_update_slice_in_dim(
        jnp.zeros((lru_width, 2 * block_width), BF),
        (grad_blocks * rows_w[6][:, None]).astype(BF),
        start,
        0,
    )
    mix_factors = [grad_mix, mix_bf, mixed, grad_pair]
    vectors = lax.dynamic_update_slice_in_dim(
        jnp.zeros((1 + tap_count, lru_width), F32), row_grads[: 1 + tap_count], start, 1
    )
    vectors = jnp.concatenate([mix_gain_rows[:1], gain_rows[:1], vectors], axis=0)
    vectors = jnp.pad(vectors, ((0, -vectors.shape[0] % 8), (0, 0)))
    if p.rests == 1:
        grad_inputs, vectors, mix_grads = final(
            grad_mixed_parts, x_own, mix_gain, grad_x_one, vectors,
            by_owner(blocks_all, p), mix_factors, p,
        )
    else:
        products = [dot_left_t(*mix_factors[:2]), dot_left_t(*mix_factors[2:])]
        products = [blocks_all, products[0], products[1][:, :part], products[1][:, part:]]
        mix_grads = [grads_out(grad.astype(BF), p) for grad in products]
        grad_mixed_own = scatter_z(grad_mixed_parts, p)
        grad_inputs = grad_x_one + norm_back(x_own.astype(F32), mix_gain, grad_mixed_own)[0]
        for exchange in (swap_core, swap_x, swap_f):
            vectors = vectors + exchange(vectors)
        for bit in (1, 2):
            vectors = vectors + move(vectors, lambda r, z, q, bit=bit: (r, z ^ bit, q))
        total = vectors
        for d in range(1, p.rests):
            total = total + shift_r(vectors, d)
        vectors = total
    vectors = lax.dynamic_slice_in_dim(vectors, p.index * rows, rows, 1)

    def mix_columns(grad):
        picked = [grad[k][:, : len(owned[k]) * block_width] for k in range(TP)]
        return jnp.concatenate(picked, axis=1).astype(F32)

    if p.rests == 1:
        share_down, share_gate, share_up = unpack(ffw_pieces, 3)
    else:
        ffw_grads = [dot_left_t(*factors[:2]), dot_left_t(*factors[2:])]
        ffw_grads = [grads_out(grad.astype(BF), p) for grad in ffw_grads]
        beside = lambda v: jnp.swapaxes(v, 0, 1).reshape(rows, -1).astype(F32)
        share_gate = beside(ffw_grads[1][:, :, :ffw_part])
        share_up = beside(ffw_grads[1][:, :, ffw_part:])
        share_down = beside(ffw_grads[0])
    shape = (micro, 1, span, width)
    return (
        mixed_out.reshape(shape),
        grad_inputs.reshape(shape),
        mix_columns(mix_grads[2]),
        mix_columns(mix_grads[3]),
        jnp.sum(mix_grads[0].astype(F32), axis=0),
        mix_columns(mix_grads[1]).T,
        share_gate,
        share_up,
        share_down.T,
        vectors[0],
        vectors[1],
        vectors[2],
        vectors[3 : 3 + tap_count].T,
    )


def solution(mesh):
    in_specs = (
        P(None, "fsdp", "seq", None),
        P(None, "fsdp", "seq", None),
        P(("fsdp", "seq"), None),
        P(("fsdp", "seq"), None),
        P(("fsdp", "seq"), None),
        P(None, ("fsdp", "seq")),
        P(("fsdp", "seq"), None),
        P(("fsdp", "seq"), None),
        P(None, ("fsdp", "seq")),
        P(("fsdp", "seq")),
        P(("fsdp", "seq")),
        P(("fsdp", "seq")),
        P(("fsdp", "seq"), None),
    )
    out_specs = (
        P(None, "fsdp", "seq", None),
        P(None, "fsdp", "seq", None),
        P(("fsdp", "seq"), None),
        P(("fsdp", "seq"), None),
        P(("fsdp", "seq"), None),
        P(None, ("fsdp", "seq")),
        P(("fsdp", "seq"), None),
        P(("fsdp", "seq"), None),
        P(None, ("fsdp", "seq")),
        P(("fsdp", "seq")),
        P(("fsdp", "seq")),
        P(("fsdp", "seq")),
        P(("fsdp", "seq"), None),
    )
    return jax.shard_map(
        on_device, mesh=mesh, in_specs=in_specs, out_specs=out_specs, check_vma=False
    )
```

profile of v0, /device:TPU:0, one launch (start us, length us, event | category | flops | bytes accessed | tf_op | source)
XLA Modules:
  0.0 677.1 jit_solution(16472980216701806089)
XLA Ops:
  1.6 2.4 collective-permute-start
  4.8 1.9 slice_bitcast_fusion
  7.3 5.2 shard_map.228
  13.5 133.4 %shard_map.229 = (bf16[2,1,4,2,2,80,2944]{6,5,4,3,2,1,0:T(8,128)(2,1)}, bf16[2,1,4,2,2,80,5760]{6,5,4,3,2,1,0:T(8,128)(2,1)}, bf16[80,5760]{1,0:T(8,128)(2,1)}, ...) custom-call(bf16[4,80,2944]{2,1,0:T(8,128)(2,1)} %get-tuple-element.77.mix_p, ...), custom_call_target="tpu_custom_call" | custom-call | tf_op jit(solution)/shard_map/pallas_call | solution.py:953
  146.9 1.7 collective-permute-start.1
  149.4 2.5 collective-permute-start.4
  151.9 18.4 %shard_map.230 = (f32[8,2560]{1,0:T(8,128)}, f32[8,768]{1,0:T(8,128)}, bf16[512,2560]{1,0:T(8,128)(2,1)}, f32[576,1536]{1,0:T(8,128)}, bf16[512,768]{1,0:T(8,128...) custom-call(bf16[576,2560]{1,0:T(8,128)(2,1)} %bitcast.86, ...), custom_call_target="tpu_custom_call" | custom-call | tf_op jit(solution)/shard_map/pallas_call | solution.py:333
  170.3 6.2 shard_map.231
  176.6 10.6 %shard_map.232 = (bf16[512,768]{1,0:T(8,128)(2,1)}, bf16[512,2560]{1,0:T(8,128)(2,1)}) custom-call(f32[576,1536]{1,0:T(8,128)} %get-tuple-element.83.pre, f32[8,768]{1,0:T(8,128)} %get-tuple-element.84.rows, f32[512,768]{1,0:T(8,128)} %get-tuple-element.85.state, f32[512,768]{1,0:T(8,128)} %get-tuple-element.86.prod, f32[8,768]{1,0:T(8,128)} %get-tuple-element.88.start, ...), custom_call_target="tpu_custom_call" | custom-call | tf_op jit(solution)/shard_map/pallas_call | solution.py:378
  188.0 2.1 constant_dynamic-slice_fusion.1
  190.0 1.6 fusion.1
  194.0 161.8 %shard_map.233 = (f32[4,32,2560]{2,1,0:T(8,128)}, bf16[4,4,32,2560]{3,2,1,0:T(8,128)(2,1)}, bf16[4,2,64,2560]{3,2,1,0:T(8,128)(2,1)}, bf16[2,1,4,2,2,80,5760]{6,...) custom-call(bf16[4,4,32,2560]{3,2,1,0:T(8,128)(2,1)} %bitcast.92, ...), custom_call_target="tpu_custom_call", output_to_operand_aliasing={{3}: (10, {})} | custom-call | tf_op jit(solution)/shard_map/pallas_call | solution.py:1267
  355.8 148.1 %shard_map.234 = (bf16[4,32,2560]{2,1,0:T(8,128)(2,1)}, f32[4,32,2560]{2,1,0:T(8,128)}, f32[8,2560]{1,0:T(8,128)}, bf16[4,4,32,2560]{3,2,1,0:T(8,128)(2,1)}, bf1...) custom-call(bf16[4,4,32,2560]{3,2,1,0:T(8,128)(2,1)} %bitcast.90, ...), custom_call_target="tpu_custom_call" | custom-call | tf_op jit(solution)/shard_map/pallas_call | solution.py:1629
  505.2 1.5 collective-permute-start.7
  506.7 1.9 collective-permute-start.8
  508.6 14.1 %shard_map.235 = (bf16[512,768]{1,0:T(8,128)(2,1)}, f32[512,768]{1,0:T(8,128)}, f32[512,768]{1,0:T(8,128)}, f32[8,768]{1,0:T(8,128)}) custom-call(bf16[512,2560]{1,0:T(8,128)(2,1)} %bitcast.78, f32[576,1536]{1,0:T(8,128)} %get-tuple-element.83.pre, f32[8,768]{1,0:T(8,128)} %get-tuple-element.84.rows, f32[512,768]{1,0:T(8,128)} %get-tuple-element.85.state, ...), custom_call_target="tpu_custom_call" | custom-call | tf_op jit(solution)/shard_map/pallas_call | solution.py:427
  522.8 5.6 shard_map.236
  528.4 9.5 %shard_map.237 = (f32[768,512]{1,0:T(8,128)}, f32[512,768]{1,0:T(8,128)}, f32[64,768]{1,0:T(8,128)}, f32[8,768]{1,0:T(8,128)}) custom-call(f32[512,768]{1,0:T(8,128)} %get-tuple-element.107.local, f32[512,768]{1,0:T(8,128)} %get-tuple-element.108.prods, f32[8,768]{1,0:T(8,128)} %get-tuple-element.111.carried, f32[512,768]{1,0:T(8,128)} %get-tuple-element.85.state, ...), custom_call_target="tpu_custom_call" | custom-call | tf_op jit(solution)/shard_map/pallas_call | solution.py:495
  537.9 1.4 collective-permute-start.5
  540.5 2.2 collective-permute-done.5
  543.4 13.5 %shard_map.238 = (bf16[512,1536]{1,0:T(8,128)(2,1)}, bf16[512,2560]{1,0:T(8,128)(2,1)}, f32[8,2560]{1,0:T(8,128)}) custom-call(bf16[512,768]{1,0:T(8,128)(2,1)} %get-tuple-element.106.gelu, f32[512,768]{1,0:T(8,128)} %get-tuple-element.113.lru, f32[64,768]{1,0:T(8,128)} %bitcast.95, f32[8,768]{1,0:T(8,128)} %get-tuple-element.84.rows, ...), custom_call_target="tpu_custom_call" | custom-call | tf_op jit(solution)/shard_map/pallas_call | solution.py:562
  558.5 102.8 %shard_map.239 = (f32[4,32,2560]{2,1,0:T(8,128)}, f32[8,2560]{1,0:T(8,128)}, bf16[4,80,512]{2,1,0:T(8,128)(2,1)}, bf16[4,80,768]{2,1,0:T(8,128)(2,1)}, bf16[4,80...) custom-call(bf16[4,4,32,2560]{3,2,1,0:T(8,128)(2,1)} %bitcast.91, ...), custom_call_target="tpu_custom_call" | custom-call | tf_op jit(solution)/shard_map/pallas_call | solution.py:1794
  661.3 1.4 slice_bitcast_fusion.5
  669.3 5.5 shard_map.240
  (67 shorter events, 20.5 us)
Async XLA Ops:
  1.6 11.0 %collective-permute-start = (bf16[2,3,2560]{2,1,0:T(4,128)(2,1)S(1)}, bf16[2,3,2560]{2,1,0:T(4,128)(2,1)S(1)}, u32[]{:S(2)}, u32[]{:S(2)}) collective-permute-start(bf16[2,3,2560]{2,1,0:T(4,128)(2,1)S(1)} %slice.130), channel_id=1, source_target_pairs={{0,1},{1,2},{2,3},{3,4},{4,5},{5,6},{6,7},{7,8},{8,9},{9,10},{10,1... | collective-permute-start | bytes 92168 | tf_op jit(solution)/shard_map/ppermute | solution.py:1950
  7.3 5.2 copy-start.1
  146.9 45.8 %collective-permute-start.1 = (bf16[80,5760]{1,0:T(8,128)(2,1)}, bf16[80,5760]{1,0:T(8,128)(2,1)S(1)}, u32[]{:S(2)}, u32[]{:S(2)}) collective-permute-start(bf16[80,5760]{1,0:T(8,128)(2,1)} %get-tuple-element.92.refs_5_), channel_id=1, source_target_pairs={{0,2},{1,3},{2,0},{3,1},{4,6},{5,7},{6,4},{7,5},{8,10},{9,11},{10,... | collective-permute-start | bytes 2764808 | tf_op jit(solution)/shard_map/ppermute | solution.py:32
  148.6 44.1 %collective-permute-start.2 = (bf16[80,5760]{1,0:T(8,128)(2,1)}, bf16[80,5760]{1,0:T(8,128)(2,1)S(1)}, u32[]{:S(2)}, u32[]{:S(2)}) collective-permute-start(bf16[80,5760]{1,0:T(8,128)(2,1)} %get-tuple-element.92.refs_5_), channel_id=1, source_target_pairs={{0,16},{16,0},{1,17},{17,1},{2,18},{18,2},{3,19},{19,3},{4,20},{20... | collective-permute-start | bytes 2764808 | tf_op jit(solution)/shard_map/ppermute | solution.py:44
  149.4 43.0 %collective-permute-start.3 = (bf16[80,5760]{1,0:T(8,128)(2,1)}, bf16[80,5760]{1,0:T(8,128)(2,1)S(1)}, u32[]{:S(2)}, u32[]{:S(2)}) collective-permute-start(bf16[80,5760]{1,0:T(8,128)(2,1)} %get-tuple-element.93), channel_id=1, source_target_pairs={{0,8},{1,9},{2,10},{3,11},{4,12},{5,13},{6,14},{7,15},{8,0},{9,1},... | collective-permute-start | bytes 2764808 | tf_op jit(solution)/shard_map/ppermute | solution.py:32
  149.4 43.3 %collective-permute-start.4 = (bf16[80,5760]{1,0:T(8,128)(2,1)}, bf16[80,5760]{1,0:T(8,128)(2,1)}, u32[]{:S(2)}, u32[]{:S(2)}) collective-permute-start(bf16[80,5760]{1,0:T(8,128)(2,1)} %get-tuple-element.94), channel_id=1, source_target_pairs={{0,12},{1,13},{2,14},{3,15},{4,0},{5,1},{6,2},{7,3},{8,4},{9,5},{1... | collective-permute-start | bytes 2764808 | tf_op jit(solution)/shard_map/ppermute | solution.py:32
  192.5 0.9 copy-start.7
  192.7 1.0 copy-start.5
  192.7 1.3 copy-start.6
  503.9 164.4 %collective-permute-start.6 = (bf16[80,5760]{1,0:T(8,128)(2,1)}, bf16[80,5760]{1,0:T(8,128)(2,1)S(1)}, u32[]{:S(2)}, u32[]{:S(2)}) collective-permute-start(bf16[80,5760]{1,0:T(8,128)(2,1)} %get-tuple-element.130), channel_id=1, source_target_pairs={{0,4},{1,5},{2,6},{3,7},{4,8},{5,9},{6,10},{7,11},{8,12},{9,13},{1... | collective-permute-start | bytes 2764808 | tf_op jit(solution)/shard_map/ppermute | solution.py:32
  505.2 163.1 %collective-permute-start.7 = (bf16[80,5760]{1,0:T(8,128)(2,1)}, bf16[80,5760]{1,0:T(8,128)(2,1)}, u32[]{:S(2)}, u32[]{:S(2)}) collective-permute-start(bf16[80,5760]{1,0:T(8,128)(2,1)} %get-tuple-element.131), channel_id=1, source_target_pairs={{0,8},{1,9},{2,10},{3,11},{4,12},{5,13},{6,14},{7,15},{8,0},{9,1},... | collective-permute-start | bytes 2764808 | tf_op jit(solution)/shard_map/ppermute | solution.py:32
  506.7 161.7 %collective-permute-start.8 = (bf16[80,5760]{1,0:T(8,128)(2,1)}, bf16[80,5760]{1,0:T(8,128)(2,1)}, u32[]{:S(2)}, u32[]{:S(2)}) collective-permute-start(bf16[80,5760]{1,0:T(8,128)(2,1)} %get-tuple-element.132), channel_id=1, source_target_pairs={{0,12},{1,13},{2,14},{3,15},{4,0},{5,1},{6,2},{7,3},{8,4},{9,5},{1... | collective-permute-start | bytes 2764808 | tf_op jit(solution)/shard_map/ppermute | solution.py:32
  537.8 2.4 copy-start.2
  537.8 2.7 copy-start.11
  537.9 4.9 collective-permute-start.5
  540.5 16.5 %copy-start = (bf16[2560,512]{1,0:T(8,128)(2,1)}, bf16[2560,512]{1,0:T(8,128)(2,1)S(1)}, u32[]{:S(2)}) copy-start(bf16[2560,512]{1,0:T(8,128)(2,1)S(1)} %fusion) | copy-start | bytes 7864324
  661.3 1.5 copy-start.9
  661.3 1.6 copy-start.10
  667.4 7.4 %copy-start.8 = (bf16[4,32,2560]{2,1,0:T(8,128)(2,1)S(1)}, bf16[4,32,2560]{2,1,0:T(8,128)(2,1)}, u32[]{:S(2)}) copy-start(bf16[4,32,2560]{2,1,0:T(8,128)(2,1)} %get-tuple-element.103) | copy-start | bytes 1966084
  668.3 7.3 %copy-start.3 = (f32[4,32,2560]{2,1,0:T(8,128)S(1)}, f32[4,32,2560]{2,1,0:T(8,128)}, u32[]{:S(2)}) copy-start(f32[4,32,2560]{2,1,0:T(8,128)} %get-tuple-element.124) | copy-start | bytes 3932164
  668.3 0.9 copy-start.4
where the time goes:
time: 684 us; the launch traced here: 677 us
  Pallas kernels  635 us (93%)
  local copies, waits for them, and re-layouts  17.5 us (3%)
  starting transfers between devices  13.4 us (2%)
    pallas_call x1, Pallas kernels, middle(): pl.pallas_call(functools.partial(middle_kernel, with_ffw), in_specs=[VMEM...  162 us
    pallas_call x1, Pallas kernels, turn(): pl.pallas_call(functools.partial(turn_kernel, count), in_specs=[VMEM] * 5...  148 us
    pallas_call x1, Pallas kernels, intake(): pl.pallas_call(intake_kernel, in_specs=[ANY] * 5, out_specs=[ANY] * 5, ou...  133 us
    pallas_call x1, Pallas kernels, final(): pl.pallas_call(final_kernel, in_specs=[VMEM] * 5 + [ANY] * 5, out_specs=[...  103 us
    pallas_call x1, Pallas kernels, recur(): pl.pallas_call(functools.partial(recur_kernel, dims), in_specs=[VMEM, ANY...  18.4 us
    pallas_call x1, Pallas kernels, recur_back(): pl.pallas_call(functools.partial(recur_back_kernel, dims), in_specs=[VMEM...  14.1 us
  transfers between devices with their start and end apart: 9, of which 3 were waited for; matrix products, arithmetic and copies ran while one was open for 3% of the time, Pallas kernels for 27%

commit v1 on v0

--- a/solution.py
+++ b/solution.py
@@ -262,89 +262,97 @@
 
 
 def recur_kernel(
-    dims, x_all, mix_w, small, rows, mixed, pre, conv, gate, state, prod, sums,
-    small_w, gl_w, block_w, mixed_all, sems,
+    dims, x_all, gelu_w, lru_w, mix_w, small, rows, mixed, pre_gelu, pre_lru, conv, gate, state,
+    prod, sums, small_w, block_w, mixed_all, sems,
 ):
     span, micro, heads, held, bw, taps = dims
-    part = held * bw
-    p = Place()
-    start = pl.multiple_of(p.z * heads // TP * bw, 128)
-    pieces = (
-        (mix_w.at[:, pl.ds(3 * part + 2 * bw, 128)], small_w),
-        (mix_w.at[:, pl.ds(0, 2 * part)], gl_w),
-        (mix_w.at[pl.ds(start, part), pl.ds(3 * part, 2 * bw)], block_w),
-    )
-    loads = [pltpu.make_async_copy(src, dst, sems.at[i]) for i, (src, dst) in enumerate(pieces)]
-    for load in loads:
-        load.start()
-    loads[0].wait()
-    row = lax.broadcasted_iota(jnp.int32, (8, 128), 0)
-    lane = lax.broadcasted_iota(jnp.int32, (8, 128), 1)
-    small[...] = dot_right_t(jnp.where(row == lane, 1.0, 0.0).astype(BF), small_w[...])
-    own = small[:, pl.ds(start, part)]
-    decay = -own[2:3]
-    feature = lax.broadcasted_iota(jnp.int32, (1, part), 1)
-    count = ((p.z + 1) * heads // TP - p.z * heads // TP) * bw
-    rows[0:1] = jnp.maximum(decay, 0.0) + jnp.log1p(jnp.exp(-jnp.abs(decay)))
-    rows[1:2] = jax.nn.sigmoid(decay)
-    rows[2 : 2 + taps] = own[3 : 3 + taps]
-    rows[6:7] = jnp.where(feature < count, 1.0, 0.0)
-    rows[7:8] = jnp.zeros((1, part), F32)
-    gain, wide, step = small[0:1], micro * (span + HALO), 16
-
-    def norm(z, _):
-        for k in range(0, wide, step):
-            vals = x_all[pl.ds(pl.multiple_of(z * wide + k, step), step)].astype(F32)
-            vals = normed(vals, gain).astype(BF)
-            mixed_all[pl.ds(pl.multiple_of(z * wide + k, step), step)] = vals
-            if k < micro * span:
-                mixed[pl.ds(pl.multiple_of(z * micro * span + k, step), step)] = vals
-        return 0
-
-    lax.fori_loop(0, TP, norm, 0)
-    loads[1].wait()
-
-    def project(h):
-        cols = pl.ds(pl.multiple_of(h * bw, 128), bw)
-        pre[:, cols] = dot_plain(mixed_all[...], gl_w[:, cols])
-
-    by_heads(2 * held, project)
-    loads[2].wait()
-
-    def one_head(h):
-        block = block_w.at[pl.ds(pl.multiple_of(h * bw, 128), bw)]
-        sums_h = sums.at[:, :, pl.ds(pl.multiple_of(h * bw, 128), bw)]
-        recur_head(
-            span, micro, columns(pre, held + h, bw), columns(rows, h, bw), block,
-            columns(conv, h, bw), columns(gate, h, 2 * bw), columns(state, h, bw),
-            columns(prod, h, bw), sums_h,
+    part, h = held * bw, pl.program_id(0)
+
+    @pl.when(h == 0)
+    def _():
+        p = Place()
+        start = pl.multiple_of(p.z * heads // TP * bw, 128)
+        pieces = (
+            (mix_w.at[:, pl.ds(3 * part + 2 * bw, 128)], small_w),
+            (mix_w.at[pl.ds(start, part), pl.ds(3 * part, 2 * bw)], block_w),
         )
-
-    by_heads(held, one_head)
+        loads = [pltpu.make_async_copy(src, dst, sems.at[i]) for i, (src, dst) in enumerate(pieces)]
+        for load in loads:
+            load.start()
+        loads[0].wait()
+        row = lax.broadcasted_iota(jnp.int32, (8, 128), 0)
+        lane = lax.broadcasted_iota(jnp.int32, (8, 128), 1)
+        small[...] = dot_right_t(jnp.where(row == lane, 1.0, 0.0).astype(BF), small_w[...])
+        own = small[:, pl.ds(start, part)]
+        decay = -own[2:3]
+        feature = lax.broadcasted_iota(jnp.int32, (1, part), 1)
+        count = ((p.z + 1) * heads // TP - p.z * heads // TP) * bw
+        rows[0:1] = jnp.maximum(decay, 0.0) + jnp.log1p(jnp.exp(-jnp.abs(decay)))
+        rows[1:2] = jax.nn.sigmoid(decay)
+        rows[2 : 2 + taps] = own[3 : 3 + taps]
+        rows[6:7] = jnp.where(feature < count, 1.0, 0.0)
+        rows[7:8] = jnp.zeros((1, part), F32)
+        gain, wide, step = small[0:1], micro * (span + HALO), 16
+
+        def norm(z, _):
+            for k in range(0, wide, step):
+                vals = x_all[pl.ds(pl.multiple_of(z * wide + k, step), step)].astype(F32)
+                vals = normed(vals, gain).astype(BF)
+                mixed_all[pl.ds(pl.multiple_of(z * wide + k, step), step)] = vals
+                if k < micro * span:
+                    mixed[pl.ds(pl.multiple_of(z * micro * span + k, step), step)] = vals
+            return 0
+
+        lax.fori_loop(0, TP, norm, 0)
+        loads[1].wait()
+
+    pre_gelu[...] = dot_plain(mixed_all[...], gelu_w[...])
+    pre_lru[...] = dot_plain(mixed_all[...], lru_w[...])
+    block = block_w.at[pl.ds(pl.multiple_of(h * bw, 128), bw)]
+    recur_head(span, micro, pre_lru, columns(rows, h, bw), block, conv, gate, state, prod, sums)
 
 
 def recur(x_all, mix_w, dims):
     span, micro, _, held, bw, _ = dims
-    part, width = held * bw, x_all.shape[1]
-    tokens = x_all.shape[0] // (span + HALO) * span
+    part, width, wide = held * bw, x_all.shape[1], x_all.shape[0]
+    tokens = wide // (span + HALO) * span
+    whole = lambda shape: pl.BlockSpec(shape, lambda h: (0, 0))
+    column = lambda rows, cols: pl.BlockSpec((rows, cols), lambda h: (0, h))
     shapes = [((8, width), F32), ((8, part), F32), ((tokens, width), BF)]
-    shapes += [((x_all.shape[0], 2 * part), F32), ((tokens, part), BF), ((tokens, 2 * part), F32)]
-    shapes += [((tokens, part), F32), ((tokens, part), F32), ((2, tokens // span, part), F32)]
+    shapes += [((wide, part), F32), ((wide, part), F32), ((tokens, part), BF)]
+    shapes += [((tokens, 2 * part), F32), ((tokens, part), F32), ((tokens, part), F32)]
+    shapes += [((2, tokens // span, part), F32)]
     return pl.pallas_call(
         functools.partial(recur_kernel, dims),
-        in_specs=[VMEM, ANY],
-        out_specs=[VMEM] * len(shapes),
+        grid=(held,),
+        in_specs=[
+            whole(x_all.shape),
+            column(width, bw),
+            pl.BlockSpec((width, bw), lambda h: (0, held + h)),
+            ANY,
+        ],
+        out_specs=[
+            whole((8, width)),
+            whole((8, part)),
+            whole((tokens, width)),
+            column(wide, bw),
+            column(wide, bw),
+            column(tokens, bw),
+            column(tokens, 2 * bw),
+            column(tokens, bw),
+            column(tokens, bw),
+            pl.BlockSpec((2, tokens // span, bw), lambda h: (0, 0, h)),
+        ],
         out_shape=[jax.ShapeDtypeStruct(*shape) for shape in shapes],
         scratch_shapes=[
             pltpu.VMEM((width, 128), BF),
-            pltpu.VMEM((width, 2 * part), BF),
             pltpu.VMEM((part, 2 * bw), BF),
             pltpu.VMEM(x_all.shape, BF),
-            pltpu.SemaphoreType.DMA((3,)),
+            pltpu.SemaphoreType.DMA((2,)),
         ],
         cost_estimate=FREE,
         compiler_params=pltpu.CompilerParams(vmem_limit_bytes=GRANT),
-    )(x_all, mix_w)
+    )(x_all, mix_w, mix_w, mix_w)
 
 
 def recur_mix_kernel(dims, pre, rows, state, prod, start, mix_w, mix, parts, out_w, sem):
@@ -390,50 +398,48 @@
 
 
 def recur_back_kernel(
-    dims, grad, pre, rows, state, prod, start, gate, mix_w, gelu, local, prods, sums, back, out_w, sem
+    dims, grad, pre, rows, state, prod, start, gate, out_w, gelu, local, prods, sums, back
 ):
-    span, micro, _, held, bw, _ = dims
-    part = held * bw
-    load = pltpu.make_async_copy(mix_w.at[:, pl.ds(2 * part, part)], out_w, sem.at[0])
-    load.start()
-    load.wait()
-
-    def one_head(h):
-        back[...] = dot_plain(grad[...], out_w[:, pl.ds(pl.multiple_of(h * bw, 128), bw)])
-        pre_h, state_h, prod_h = columns(pre, h, bw), columns(state, h, bw), columns(prod, h, bw)
-        rows_h, start_h, gate_h = columns(rows, h, bw), columns(start, h, bw), columns(gate, h, 2 * bw)
-        gelu_h, local_h = columns(gelu, h, bw), columns(local, h, bw)
-        prods_h, sums_h = columns(prods, h, bw), columns(sums, h, bw)
-        soft = rows_h[0:1]
-        for i in range(back.shape[0] // span):
-            here = pl.ds(i * span, span)
-            act, slope = gelu_pair(pre_h[main_rows(i, span, micro)])
-            states = state_h[here] + prod_h[here] * start_h[i : i + 1]
-            gelu_h[here] = (back[here] * states * slope * rows_h[6:7]).astype(BF)
-            _, _, decay, _, _ = gate_values(gate_h[here], soft)
-            row = lax.broadcasted_iota(jnp.int32, decay.shape, 0)
-            later = jnp.where(row < span - 1, pltpu.roll(decay, span - 1, 0), 1.0)
-            later, adjoint = span_scan(later, back[here] * act, True)
-            local_h[here] = adjoint
-            prods_h[here] = later
-            sums_h[i : i + 1] = decay[:1] * adjoint[:1]
-
-    by_heads(held, one_head)
+    span, micro = dims[:2]
+    soft = rows[0:1]
+    back[...] = dot_plain(grad[...], out_w[...])
+    for i in range(back.shape[0] // span):
+        here = pl.ds(i * span, span)
+        act, slope = gelu_pair(pre[main_rows(i, span, micro)])
+        states = state[here] + prod[here] * start[i : i + 1]
+        gelu[here] = (back[here] * states * slope * rows[6:7]).astype(BF)
+        _, _, decay, _, _ = gate_values(gate[here], soft)
+        row = lax.broadcasted_iota(jnp.int32, decay.shape, 0)
+        later = jnp.where(row < span - 1, pltpu.roll(decay, span - 1, 0), 1.0)
+        later, adjoint = span_scan(later, back[here] * act, True)
+        local[here] = adjoint
+        prods[here] = later
+        sums[i : i + 1] = decay[:1] * adjoint[:1]
 
 
 def recur_back(grad, pre, rows, state, prod, start, gate, mix_w, dims):
     tokens, part = state.shape
+    held, bw = dims[3:5]
+    column = lambda h: (0, h)
+    whole = pl.BlockSpec((tokens, bw), column)
+    ends = pl.BlockSpec((start.shape[0], bw), column)
     shapes = [((tokens, part), BF), ((tokens, part), F32), ((tokens, part), F32), (start.shape, F32)]
     return pl.pallas_call(
         functools.partial(recur_back_kernel, dims),
-        in_specs=[VMEM] * 7 + [ANY],
-        out_specs=[VMEM] * 4,
+        grid=(held,),
+        in_specs=[
+            pl.BlockSpec(grad.shape, lambda h: (0, 0)),
+            pl.BlockSpec((pre.shape[0], bw), column),
+            pl.BlockSpec((8, bw), column),
+            whole,
+            whole,
+            ends,
+            pl.BlockSpec((tokens, 2 * bw), column),
+            pl.BlockSpec((mix_w.shape[0], bw), lambda h: (0, 2 * held + h)),
+        ],
+        out_specs=[whole, whole, whole, ends],
         out_shape=[jax.ShapeDtypeStruct(*shape) for shape in shapes],
-        scratch_shapes=[
-            pltpu.VMEM((tokens, dims[4]), F32),
-            pltpu.VMEM((mix_w.shape[0], part), BF),
-            pltpu.SemaphoreType.DMA((1,)),
-        ],
+        scratch_shapes=[pltpu.VMEM((tokens, bw), F32)],
         cost_estimate=FREE,
         compiler_params=pltpu.CompilerParams(vmem_limit_bytes=GRANT),
     )(grad, pre, rows, state, prod, start, gate, mix_w)
@@ -504,7 +510,7 @@
             ends,
             pl.BlockSpec((tokens, 2 * bw), column),
             whole,
-            pl.BlockSpec((pre.shape[0], bw), lambda h: (0, held + h)),
+            pl.BlockSpec((pre.shape[0], bw), column),
             pl.BlockSpec((8, bw), column),
             pl.BlockSpec((1, bw, 2 * bw), lambda h: (h, 0, 0)),
         ],
@@ -526,49 +532,58 @@
     )(local, prods, carried, state, prod, start, gate, conv, pre, rows, blocks)
 
 
-def recur_in_kernel(
-    dims, gelu, lru, spill, rows, small, mixed, mix_w, pair, parts, gains, gl_w, sem
-):
+def recur_in_kernel(dims, gelu, lru, spill, rows, small, mixed, mix_w, pair, parts, gains):
     span, _, _, held, bw, _ = dims
     part = held * bw
-    load = pltpu.make_async_copy(mix_w.at[:, pl.ds(0, 2 * part)], gl_w, sem.at[0])
-    load.start()
-    pair[:, :part] = gelu[...]
-
-    def one_head(h):
-        lru_h, spill_h, own = columns(lru, h, bw), columns(spill, h, bw), columns(rows, h, bw)[6:7]
-        for i in range(lru.shape[0] // span):
-            vals = lru_h[pl.ds(i * span, span)]
-            late = vals[span - HALO :] + spill_h[pl.ds(i * HALO, HALO)]
-            vals = jnp.concatenate([vals[: span - HALO], late], axis=0) * own
-            pair[pl.ds(i * span, span), pl.ds(pl.multiple_of((held + h) * bw, 128), bw)] = vals.astype(BF)
-
-    by_heads(held, one_head)
-    load.wait()
-
-    def project(j):
-        cols = pl.ds(pl.multiple_of(j * 256, 256), 256)
-        grad = dot_right_t(pair[...], gl_w[cols])
-        parts[:, cols] = grad.astype(BF)
-        gain = jnp.sum(grad * mixed[:, cols].astype(F32), axis=0, keepdims=True)
-        gains[0:1, cols] = gain / small[0:1, cols]
-
-    by_heads(gl_w.shape[0] // 256, project)
+
+    @pl.when(pl.program_id(0) == 0)
+    def _():
+        pair[:, :part] = gelu[...]
+
+        def one_head(h):
+            lru_h, spill_h, own = columns(lru, h, bw), columns(spill, h, bw), columns(rows, h, bw)[6:7]
+            cols = pl.ds(pl.multiple_of((held + h) * bw, 128), bw)
+            for i in range(lru.shape[0] // span):
+                vals = lru_h[pl.ds(i * span, span)]
+                late = vals[span - HALO :] + spill_h[pl.ds(i * HALO, HALO)]
+                vals = jnp.concatenate([vals[: span - HALO], late], axis=0) * own
+                pair[pl.ds(i * span, span), cols] = vals.astype(BF)
+
+        by_heads(held, one_head)
+
+    grad = dot_right_t(pair[...], mix_w[...])
+    parts[...] = grad.astype(BF)
+    gain = jnp.sum(grad * mixed[...].astype(F32), axis=0, keepdims=True)
+    gains[0:1] = gain / small[0:1]
 
 
 def recur_in(gelu, lru, spill, rows, small, mixed, mix_w, dims):
     tokens, part = gelu.shape
-    width = mix_w.shape[0]
+    width, chunk = mix_w.shape[0], 256
+    whole = lambda v: pl.BlockSpec(v.shape, lambda j: (0, 0))
+    column = lambda j: (0, j)
     return pl.pallas_call(
         functools.partial(recur_in_kernel, dims),
-        in_specs=[VMEM] * 6 + [ANY],
-        out_specs=[VMEM] * 3,
+        grid=(width // chunk,),
+        in_specs=[
+            whole(gelu),
+            whole(lru),
+            whole(spill),
+            whole(rows),
+            pl.BlockSpec((8, chunk), column),
+            pl.BlockSpec((tokens, chunk), column),
+            pl.BlockSpec((chunk, 2 * part), lambda j: (j, 0)),
+        ],
+        out_specs=[
+            pl.BlockSpec((tokens, 2 * part), lambda j: (0, 0)),
+            pl.BlockSpec((tokens, chunk), column),
+            pl.BlockSpec((8, chunk), column),
+        ],
         out_shape=[
             jax.ShapeDtypeStruct((tokens, 2 * part), BF),
             jax.ShapeDtypeStruct((tokens, width), BF),
             jax.ShapeDtypeStruct((8, width), F32),
         ],
-        scratch_shapes=[pltpu.VMEM((width, 2 * part), BF), pltpu.SemaphoreType.DMA((1,))],
         cost_estimate=FREE,
         compiler_params=pltpu.CompilerParams(vmem_limit_bytes=GRANT),
     )(gelu, lru, spill, rows, small, mixed, mix_w)
@@ -1475,17 +1490,22 @@
     parts, out_parts, x_one, cot, gain = refs[:5]
     factors, refs = refs[5 : 5 + (4 if count else 0)], refs[5 + (4 if count else 0) :]
     mixed_out, grad_x_one, grad_gain, mix_all = refs[:4]
-    pieces, refs = refs[4 : 4 + TP], refs[4 + TP :]
+    pieces, downs, refs = refs[4 : 4 + TP], refs[4 + TP : 4 + 2 * TP], refs[4 + 2 * TP :]
     grads, cores, refs = refs[:count], refs[count : 2 * count], refs[2 * count :]
-    own, local, gu0, gu1, gd0, gd1 = refs[:6]
+    own, local, zs, zr, gu0, gu1, gd0, gd1 = refs[:8]
     p = Place()
-    line, late = LineSum(p, parts, refs[6:14]), LineSum(p, out_parts, refs[14:22])
-    folds = folds_of(p, grads, cores, refs[22 : 22 + 12 * count])
+    line, late = LineSum(p, parts, refs[8:16]), LineSum(p, out_parts, refs[16:24])
+    folds = folds_of(p, grads, cores, refs[24 : 24 + 12 * count])
     out = Gather(p, mix_all, (gu0, gu1), (gd0, gd1))
     halves, rows = parts.shape[1:3]
     line.clear()
     late.clear()
-    greet_line(p, (*folds[0].to, folds[0].to_c) if folds else ())
+    to_z = [device(p, z=(p.z + d) % TP) for d in range(TP)]
+    started = []
+    if folds:
+        greet(to_z[1:] + [*folds[0].to, folds[0].to_c])
+    else:
+        greet_line(p)
     stays = []
 
     def stay(src, dst):
@@ -1494,7 +1514,7 @@
         stays.append(copy)
 
     if folds:
-        left, right, turned, buffers, chunk_sems, load_sems = refs[22 + 12 * count :]
+        left, right, turned, buffers, chunk_sems, load_sems = refs[24 + 12 * count :]
         part = factors[1].shape[1]
         outers = [
             Outer(grads[m], left, right.at[:, pl.ds(m // 2 * part, part)], turned, buffers, chunk_sems)
@@ -1574,6 +1594,12 @@
         late.step(2, h)
     if folds:
         join(down, 6, 7)
+        down.finish()
+        stay(down.result(p.z), downs[0])
+        for d in (1, 3, 2):
+            copy = copy_to(down.result((p.z + d) % TP), downs[d], (zs, zr), (d,), to_z[d])
+            copy.start()
+            started.append(copy)
         join(up, 4, 5)
         join(gate, 6, 7)
     for h in range(halves):
@@ -1591,13 +1617,15 @@
             mixed_out[h, at] = (x_one[h, at] + late.total(h, at)).astype(BF)
 
         by_rows(rows, store)
-    offset = 0
-    for fold in folds:
+    for m, fold in enumerate(folds[1:]):
         fold.finish()
-        cols = fold.grad.shape[-1]
         for d in range(TP):
-            stay(fold.result((p.z + d) % TP), pieces[d].at[:, pl.ds(offset, cols)])
-        offset += cols
+            stay(fold.result((p.z + d) % TP), pieces[d].at[:, pl.ds(m * part, part)])
+    if folds:
+        for d in range(1, TP):
+            copy_to(downs[d], downs[d], (zs, zr), (d,), to_z[1]).wait_recv()
+    for copy in started:
+        copy.wait_send()
     for fold in folds:
         fold.close()
     line.close()
@@ -1613,7 +1641,8 @@
     sizes = [factors[1].shape[1]] * count if factors else []
     grads = [jax.ShapeDtypeStruct((p.fs, 1, TP, 2, 2, rows, size), BF) for size in sizes]
     folded = [Fold.shapes(grad, True) for grad in grads]
-    piece = jax.ShapeDtypeStruct((rows, sum(sizes)) if factors else (16, 128), BF)
+    piece = jax.ShapeDtypeStruct((rows, 2 * sizes[0]) if factors else (16, 128), BF)
+    down = jax.ShapeDtypeStruct((rows, sizes[0]) if factors else (16, 128), BF)
     extra = []
     if factors:
         assert all(size % GRAD_CHUNK == 0 for size in sizes)
@@ -1629,19 +1658,21 @@
     results = pl.pallas_call(
         functools.partial(turn_kernel, count),
         in_specs=[VMEM] * 5 + [ANY] * len(factors),
-        out_specs=[VMEM, VMEM, VMEM, ANY] + [ANY] * (TP + 2 * count),
+        out_specs=[VMEM, VMEM, VMEM, ANY] + [ANY] * (2 * TP + 2 * count),
         out_shape=[
             jax.ShapeDtypeStruct(shape[1:], BF),
             jax.ShapeDtypeStruct(shape[1:], F32),
             jax.ShapeDtypeStruct((8, width), F32),
             jax.ShapeDtypeStruct(shape, BF),
             *[piece] * TP,
+            *[down] * TP,
             *grads,
             *(cores for cores, _ in folded),
         ],
         scratch_shapes=[
             pltpu.VMEM(shape[1:], BF),
-            pltpu.SemaphoreType.DMA((shape[1] + TP * count,)),
+            pltpu.SemaphoreType.DMA((shape[1] + 2 * TP + 1,)),
+            *pairs(TP),
             *pairs(TP - 1, shape[1]),
             *pairs(TP - 1, shape[1]),
             *LineSum.scratch(shape),
@@ -1653,7 +1684,7 @@
             collective_id=2, has_side_effects=True, vmem_limit_bytes=GRANT
         ),
     )(parts, out_parts, x_one, cot, gain, *factors)
-    return results[: 4 + TP]
+    return results[:4], results[4 : 4 + TP], results[4 + TP : 4 + 2 * TP]
 
 
 def final_kernel(*refs):
@@ -1730,28 +1761,33 @@
     vector(0).start()
     folds[0].begin()
     line_step(3)
+    join(0, 0, 1, 2, 3)
     load(0)
     outer(1)
     load(1)
-    join(0, 0, 1, 2, 3)
-    outer(2)
     join(0, 4, 5)
     join(1, 0, 1)
     folds[0].middle()
     join(1, 2, 3)
-    outer(3)
+    outer(2)
     line_step(2)
     next_vector(0)
-    for m in (1, 2):
-        join(m - 1, 6, 7)
-        join(m, 4, 5)
-        join(m + 1, 0, 1)
-        folds[m].middle()
-        join(m + 1, 2, 3)
-        if m == 1:
-            line_step(1)
-        next_vector(m)
-        send_on(m - 1)
+    join(0, 6, 7)
+    join(1, 4, 5)
+    join(2, 0, 1)
+    folds[1].middle()
+    join(2, 2, 3)
+    outer(3)
+    line_step(1)
+    next_vector(1)
+    send_on(0)
+    join(1, 6, 7)
+    join(2, 4, 5)
+    join(3, 0, 1)
+    folds[2].middle()
+    join(3, 2, 3)
+    next_vector(2)
+    send_on(1)
     join(2, 6, 7)
     join(3, 4, 5)
     folds[3].middle()
@@ -1816,6 +1852,7 @@
             *LineSum.scratch(shape),
             *(item for scratch in folded for item in scratch),
         ],
+        cost_estimate=FREE,
         compiler_params=pltpu.CompilerParams(
             collective_id=3, has_side_effects=True, vmem_limit_bytes=GRANT
         ),
@@ -1878,24 +1915,55 @@
     )(*((sums, known) if backward else (sums,)))
 
 
-def unpack_kernel(own, one, two, three, *outs):
+def unpack_kernel(count, *refs):
     p = Place()
-    part = own.shape[1] // len(outs)
-    for d, piece in enumerate((own, one, two, three)):
-        cols = pl.ds(pl.multiple_of((p.z - d) % TP * part, 128), part)
-        for i, out in enumerate(outs):
-            out[:, cols] = piece[:, i * part : (i + 1) * part].astype(F32)
-
-
-def unpack(pieces, count):
-    rows, cols = pieces[0].shape
+    pieces, outs = refs[: TP * len(count)], refs[TP * len(count) :]
+    for d in range(TP):
+        first = 0
+        for m, parts in enumerate(count):
+            piece = pieces[m * TP + d]
+            part = piece.shape[1] // parts
+            cols = pl.ds(pl.multiple_of((p.z - d) % TP * part, 128), part)
+            for i in range(parts):
+                outs[first + i][:, cols] = piece[:, i * part : (i + 1) * part].astype(F32)
+            first += parts
+
+
+def unpack(groups, count):
+    shapes = []
+    for pieces, parts in zip(groups, count):
+        rows, cols = pieces[0].shape
+        shapes += [jax.ShapeDtypeStruct((rows, cols // parts * TP), F32)] * parts
     return pl.pallas_call(
-        unpack_kernel,
-        in_specs=[VMEM] * TP,
-        out_specs=[VMEM] * count,
-        out_shape=[jax.ShapeDtypeStruct((rows, cols // count * TP), F32)] * count,
+        functools.partial(unpack_kernel, count),
+        in_specs=[VMEM] * (TP * len(groups)),
+        out_specs=[VMEM] * len(shapes),
+        out_shape=shapes,
         compiler_params=pltpu.CompilerParams(vmem_limit_bytes=GRANT),
-    )(*pieces)
+    )(*(piece for pieces in groups for piece in pieces))
+
+
+def unpack_mix_kernel(spans, *refs):
+    (blocks, *mix), (blocks_out, *mix_out) = refs[:4], refs[4:]
+    total = blocks[0].astype(F32)
+    for k in range(1, TP):
+        total = total + blocks[k].astype(F32)
+    blocks_out[...] = total
+    for piece, out in zip(mix, mix_out):
+        for k, (start, count) in enumerate(spans):
+            out[:, start : start + count] = piece[k, :, :count].astype(F32)
+
+
+def unpack_mix(mix, spans):
+    wide = spans[-1][0] + spans[-1][1]
+    shapes = [mix[0].shape[1:]] + [(mix[0].shape[1], wide)] * 3
+    return pl.pallas_call(
+        functools.partial(unpack_mix_kernel, spans),
+        in_specs=[VMEM] * 4,
+        out_specs=[VMEM] * 4,
+        out_shape=[jax.ShapeDtypeStruct(shape, F32) for shape in shapes],
+        compiler_params=pltpu.CompilerParams(vmem_limit_bytes=GRANT),
+    )(*mix)
 
 
 def geglu(gate_vals, up_vals):
@@ -1977,7 +2045,7 @@
         x_all, passed, ffw_w = gather_z(x_wide, p), None, None
         cot_first = gather_z(cot_halves[:1], p)
     dims = (span, micro, heads, held, block_width, tap_count)
-    small_w, rows_w, mixed, pre, conv, gate, state, prod, sums = recur(
+    small_w, rows_w, mixed, pre, pre_lru, conv, gate, state, prod, sums = recur(
         x_all.reshape(-1, width), mix_w, dims
     )
     mix_gain, ffw_gain = small_w[0:1], small_w[1:2]
@@ -2017,12 +2085,11 @@
         grad_in_parts = dot_right_t(grad_gate_up, gate_up_w).astype(BF)
     ffw_parts, grad_in_parts = ffw_parts.reshape(blocked), grad_in_parts.reshape(blocked)
     factors = [cot_all, hidden_bf, ffw_bf, grad_gate_up]
-    mixed_out, grad_x_one, gain_rows, grad_mix, *ffw_pieces = turn(
+    (mixed_out, grad_x_one, gain_rows, grad_mix), ffw_pieces, down_pieces = turn(
         grad_in_parts, ffw_parts, x_one, cot_own, ffw_gain, factors * one, p
     )
     if p.rests == 1:
-        for d in (1, 3, 2):
-            ffw_pieces[d] = shift_z(ffw_pieces[d], d)
+        ffw_pieces = [shift_z(piece, d) if d else piece for d, piece in enumerate(ffw_pieces)]
     grad_mix = grad_mix.reshape(-1, width)
 
     grad_gelu_bf, local_back, prod_back, back_sums = recur_back(
@@ -2039,7 +2106,7 @@
         carried = own_spans(jnp.stack(carries[::-1]), p).reshape(-1, part)
     block_mats = lax.dynamic_slice(mix_w, (start, 3 * part), (part, 2 * block_width))
     grad_blocks, grad_lru, spill, row_grads = recur_grad(
-        local_back, prod_back, carried, state, prod, state_in, gate, conv, pre, rows_w,
+        local_back, prod_back, carried, state, prod, state_in, gate, conv, pre_lru, rows_w,
         block_mats.reshape(held, block_width, 2 * block_width), dims,
     )
     spill = spill.reshape(TP, micro, HALO, part)
@@ -2088,12 +2155,10 @@
         vectors = total
     vectors = lax.dynamic_slice_in_dim(vectors, p.index * rows, rows, 1)
 
-    def mix_columns(grad):
-        picked = [grad[k][:, : len(owned[k]) * block_width] for k in range(TP)]
-        return jnp.concatenate(picked, axis=1).astype(F32)
-
     if p.rests == 1:
-        share_down, share_gate, share_up = unpack(ffw_pieces, 3)
+        spans = [(first[k] * block_width, len(owned[k]) * block_width) for k in range(TP)]
+        share_blocks, share_out, share_gelu, share_lru = unpack_mix(mix_grads, spans)
+        share_gate, share_up, share_down = unpack((ffw_pieces, down_pieces), (2, 1))
     else:
         ffw_grads = [dot_left_t(*factors[:2]), dot_left_t(*factors[2:])]
         ffw_grads = [grads_out(grad.astype(BF), p) for grad in ffw_grads]
@@ -2101,14 +2166,21 @@
         share_gate = beside(ffw_grads[1][:, :, :ffw_part])
         share_up = beside(ffw_grads[1][:, :, ffw_part:])
         share_down = beside(ffw_grads[0])
+
+        def mix_columns(grad):
+            picked = [grad[k][:, : len(owned[k]) * block_width] for k in range(TP)]
+            return jnp.concatenate(picked, axis=1).astype(F32)
+
+        share_blocks = jnp.sum(mix_grads[0].astype(F32), axis=0)
+        share_out, share_gelu, share_lru = (mix_columns(grad) for grad in mix_grads[1:])
     shape = (micro, 1, span, width)
     return (
         mixed_out.reshape(shape),
         grad_inputs.reshape(shape),
-        mix_columns(mix_grads[2]),
-        mix_columns(mix_grads[3]),
-        jnp.sum(mix_grads[0].astype(F32), axis=0),
-        mix_columns(mix_grads[1]).T,
+        share_gelu,
+        share_lru,
+        share_blocks,
+        share_out.T,
         share_gate,
         share_up,
         share_down.T,

time: 684 us -> 679 us (level)
  Pallas kernels: 635 us -> 626 us
    pallas_call x4 -> x5, Pallas kernels: 51.5 us -> 47.9 us  [the longest x1 16.6 us: recur(): pl.pallas_call(functools.partial(recur_kernel, dims), grid=(held,), in_sp...]
  transfers between devices with their start and end apart: 9 -> 9, of which waited for: 3 -> 3; matrix products, arithmetic and copies ran while one was open for 3% -> 2% of each run, Pallas kernels for 27% -> 26%
where the time goes in v1:
time: 679 us; the launch traced here: 672 us
  Pallas kernels  626 us (92%)
  starting transfers between devices  19.6 us (3%)
  local copies, waits for them, and re-layouts  16.2 us (2%)
    pallas_call x1, Pallas kernels, middle(): pl.pallas_call(functools.partial(middle_kernel, with_ffw), in_specs=[VMEM...  162 us
    pallas_call x1, Pallas kernels, turn(): pl.pallas_call(functools.partial(turn_kernel, count), in_specs=[VMEM] * 5...  149 us
    pallas_call x1, Pallas kernels, intake(): pl.pallas_call(intake_kernel, in_specs=[ANY] * 5, out_specs=[ANY] * 5, ou...  133 us
    pallas_call x1, Pallas kernels, final(): pl.pallas_call(final_kernel, in_specs=[VMEM] * 5 + [ANY] * 5, out_specs=[...  97.5 us
    pallas_call x1, Pallas kernels, recur(): pl.pallas_call(functools.partial(recur_kernel, dims), grid=(held,), in_sp...  16.6 us
    ppermute x7, starting transfers between devices, move(): return lax.ppermute(value, 'seq', pairs)  16.4 us
  transfers between devices with their start and end apart: 9, of which 3 were waited for; matrix products, arithmetic and copies ran while one was open for 2% of the time, Pallas kernels for 26%

profile of v1, /device:TPU:0, one launch (start us, length us, event | category | flops | bytes accessed | tf_op | source)
XLA Modules:
  0.0 672.3 jit_solution(12107683124844583415)
XLA Ops:
  1.6 2.4 collective-permute-start
  4.8 1.9 slice_bitcast_fusion
  7.3 5.2 shard_map.228
  13.5 133.4 %shard_map.229 = (bf16[2,1,4,2,2,80,2944]{6,5,4,3,2,1,0:T(8,128)(2,1)}, bf16[2,1,4,2,2,80,5760]{6,5,4,3,2,1,0:T(8,128)(2,1)}, bf16[80,5760]{1,0:T(8,128)(2,1)}, ...) custom-call(bf16[4,80,2944]{2,1,0:T(8,128)(2,1)} %get-tuple-element.86.mix_p, ...), custom_call_target="tpu_custom_call" | custom-call | tf_op jit(solution)/shard_map/pallas_call | solution.py:968
  146.9 1.7 collective-permute-start.1
  149.4 2.5 collective-permute-start.4
  151.9 16.6 %shard_map.230 = (f32[8,2560]{1,0:T(8,128)}, f32[8,768]{1,0:T(8,128)}, bf16[512,2560]{1,0:T(8,128)(2,1)}, f32[576,768]{1,0:T(8,128)}, f32[576,768]{1,0:T(8,128)}...) custom-call(bf16[576,2560]{1,0:T(8,128)(2,1)} %bitcast.63, ...), custom_call_target="tpu_custom_call" | custom-call | tf_op jit(solution)/shard_map/pallas_call | solution.py:325
  168.5 6.2 shard_map.231
  174.7 10.1 %shard_map.232 = (bf16[512,768]{1,0:T(8,128)(2,1)}, bf16[512,2560]{1,0:T(8,128)(2,1)}) custom-call(f32[576,768]{1,0:T(8,128)} %get-tuple-element.92.pre, f32[8,768]{1,0:T(8,128)} %get-tuple-element.93.rows, f32[512,768]{1,0:T(8,128)} %get-tuple-element.94.state, f32[512,768]{1,0:T(8,128)} %get-tuple-element.95.prod, f32[8,768]{1,0:T(8,128)} %get-tuple-element.97.start, ...), custom_call_target="tpu_custom_call" | custom-call | tf_op jit(solution)/shard_map/pallas_call | solution.py:386
  185.6 2.1 constant_dynamic-slice_fusion.1
  187.7 1.6 fusion.1
  189.3 3.2 collective-permute-done.3.refs_8_
  194.0 161.9 %shard_map.233 = (f32[4,32,2560]{2,1,0:T(8,128)}, bf16[4,4,32,2560]{3,2,1,0:T(8,128)(2,1)}, bf16[4,2,64,2560]{3,2,1,0:T(8,128)(2,1)}, bf16[2,1,4,2,2,80,5760]{6,...) custom-call(bf16[4,4,32,2560]{3,2,1,0:T(8,128)(2,1)} %bitcast.69, ...), custom_call_target="tpu_custom_call", output_to_operand_aliasing={{3}: (10, {})} | custom-call | tf_op jit(solution)/shard_map/pallas_call | solution.py:1282
  355.9 149.2 %shard_map.234 = (bf16[4,32,2560]{2,1,0:T(8,128)(2,1)}, f32[4,32,2560]{2,1,0:T(8,128)}, f32[8,2560]{1,0:T(8,128)}, bf16[4,4,32,2560]{3,2,1,0:T(8,128)(2,1)}, bf1...) custom-call(bf16[4,4,32,2560]{3,2,1,0:T(8,128)(2,1)} %bitcast.67, ...), custom_call_target="tpu_custom_call" | custom-call | tf_op jit(solution)/shard_map/pallas_call | solution.py:1658
  505.1 7.5 %collective-permute-start.6 = (bf16[80,3840]{1,0:T(8,128)(2,1)}, bf16[80,3840]{1,0:T(8,128)(2,1)S(1)}, u32[]{:S(2)}, u32[]{:S(2)}) collective-permute-start(bf16[80,3840]{1,0:T(8,128)(2,1)} %get-tuple-element.144), channel_id=1, source_target_pairs={{0,4},{1,5},{2,6},{3,7},{4,8},{5,9},{6,10},{7,11},{8,12},{9,13},{1... | collective-permute-start | bytes 1843208 | tf_op jit(solution)/shard_map/ppermute | solution.py:32
  513.1 2.8 collective-permute-start.8
  515.9 10.4 %shard_map.235 = (bf16[512,768]{1,0:T(8,128)(2,1)}, f32[512,768]{1,0:T(8,128)}, f32[512,768]{1,0:T(8,128)}, f32[8,768]{1,0:T(8,128)}) custom-call(bf16[512,2560]{1,0:T(8,128)(2,1)} %bitcast.56, f32[576,768]{1,0:T(8,128)} %get-tuple-element.92.pre, f32[8,768]{1,0:T(8,128)} %get-tuple-element.93.rows, f32[512,768]{1,0:T(8,128)} %get-tuple-element.94.state, ...), custom_call_target="tpu_custom_call" | custom-call | tf_op jit(solution)/shard_map/pallas_call | solution.py:427
  526.3 5.6 shard_map.236
  531.9 9.4 %shard_map.237 = (f32[768,512]{1,0:T(8,128)}, f32[512,768]{1,0:T(8,128)}, f32[64,768]{1,0:T(8,128)}, f32[8,768]{1,0:T(8,128)}) custom-call(f32[512,768]{1,0:T(8,128)} %get-tuple-element.116.local, f32[512,768]{1,0:T(8,128)} %get-tuple-element.117.prods, f32[8,768]{1,0:T(8,128)} %get-tuple-element.120.carried, f32[512,768]{1,0:T(8,128)} %get-tuple-element.94.state, ...), custom_call_target="tpu_custom_call" | custom-call | tf_op jit(solution)/shard_map/pallas_call | solution.py:501
  544.1 2.2 collective-permute-done.5
  547.0 12.4 %shard_map.238 = (bf16[512,1536]{1,0:T(8,128)(2,1)}, bf16[512,2560]{1,0:T(8,128)(2,1)}, f32[8,2560]{1,0:T(8,128)}) custom-call(bf16[512,768]{1,0:T(8,128)(2,1)} %get-tuple-element.115.gelu, f32[512,768]{1,0:T(8,128)} %get-tuple-element.123.lru, f32[64,768]{1,0:T(8,128)} %bitcast.72, f32[8,768]{1,0:T(8,128)} %get-tuple-element.93.rows, ...), custom_call_target="tpu_custom_call" | custom-call | tf_op jit(solution)/shard_map/pallas_call | solution.py:565
  561.0 97.5 %shard_map.239 = (f32[4,32,2560]{2,1,0:T(8,128)}, f32[8,2560]{1,0:T(8,128)}, bf16[4,80,512]{2,1,0:T(8,128)(2,1)}, bf16[4,80,768]{2,1,0:T(8,128)(2,1)}, bf16[4,80...) custom-call(bf16[4,4,32,2560]{3,2,1,0:T(8,128)(2,1)} %bitcast.68, ...), custom_call_target="tpu_custom_call" | custom-call | tf_op jit(solution)/shard_map/pallas_call | solution.py:1830
  658.5 3.0 shard_map.240
  664.5 5.5 shard_map.241
  (54 shorter events, 16.8 us)
Async XLA Ops:
  1.6 10.9 %collective-permute-start = (bf16[2,3,2560]{2,1,0:T(4,128)(2,1)S(1)}, bf16[2,3,2560]{2,1,0:T(4,128)(2,1)S(1)}, u32[]{:S(2)}, u32[]{:S(2)}) collective-permute-start(bf16[2,3,2560]{2,1,0:T(4,128)(2,1)S(1)} %slice.58), channel_id=1, source_target_pairs={{0,1},{1,2},{2,3},{3,4},{4,5},{5,6},{6,7},{7,8},{8,9},{9,10},{10,1... | collective-permute-start | bytes 92168 | tf_op jit(solution)/shard_map/ppermute | solution.py:2018
  7.3 5.2 copy-start.1
  146.9 45.8 %collective-permute-start.1 = (bf16[80,5760]{1,0:T(8,128)(2,1)}, bf16[80,5760]{1,0:T(8,128)(2,1)S(1)}, u32[]{:S(2)}, u32[]{:S(2)}) collective-permute-start(bf16[80,5760]{1,0:T(8,128)(2,1)} %get-tuple-element.101.refs_5_), channel_id=1, source_target_pairs={{0,2},{1,3},{2,0},{3,1},{4,6},{5,7},{6,4},{7,5},{8,10},{9,11},{10,... | collective-permute-start | bytes 2764808 | tf_op jit(solution)/shard_map/ppermute | solution.py:32
  148.6 44.1 %collective-permute-start.2 = (bf16[80,5760]{1,0:T(8,128)(2,1)}, bf16[80,5760]{1,0:T(8,128)(2,1)S(1)}, u32[]{:S(2)}, u32[]{:S(2)}) collective-permute-start(bf16[80,5760]{1,0:T(8,128)(2,1)} %get-tuple-element.101.refs_5_), channel_id=1, source_target_pairs={{0,16},{16,0},{1,17},{17,1},{2,18},{18,2},{3,19},{19,3},{4,20},{20... | collective-permute-start | bytes 2764808 | tf_op jit(solution)/shard_map/ppermute | solution.py:44
  149.4 43.0 %collective-permute-start.3 = (bf16[80,5760]{1,0:T(8,128)(2,1)}, bf16[80,5760]{1,0:T(8,128)(2,1)S(1)}, u32[]{:S(2)}, u32[]{:S(2)}) collective-permute-start(bf16[80,5760]{1,0:T(8,128)(2,1)} %get-tuple-element.102), channel_id=1, source_target_pairs={{0,8},{1,9},{2,10},{3,11},{4,12},{5,13},{6,14},{7,15},{8,0},{9,1},... | collective-permute-start | bytes 2764808 | tf_op jit(solution)/shard_map/ppermute | solution.py:32
  149.4 43.3 %collective-permute-start.4 = (bf16[80,5760]{1,0:T(8,128)(2,1)}, bf16[80,5760]{1,0:T(8,128)(2,1)}, u32[]{:S(2)}, u32[]{:S(2)}) collective-permute-start(bf16[80,5760]{1,0:T(8,128)(2,1)} %get-tuple-element.103), channel_id=1, source_target_pairs={{0,12},{1,13},{2,14},{3,15},{4,0},{5,1},{6,2},{7,3},{8,4},{9,5},{1... | collective-permute-start | bytes 2764808 | tf_op jit(solution)/shard_map/ppermute | solution.py:32
  192.5 0.9 copy-start.6
  192.7 1.0 copy-start.4
  192.7 1.3 copy-start.5
  505.1 158.4 %collective-permute-start.6 = (bf16[80,3840]{1,0:T(8,128)(2,1)}, bf16[80,3840]{1,0:T(8,128)(2,1)S(1)}, u32[]{:S(2)}, u32[]{:S(2)}) collective-permute-start(bf16[80,3840]{1,0:T(8,128)(2,1)} %get-tuple-element.144), channel_id=1, source_target_pairs={{0,4},{1,5},{2,6},{3,7},{4,8},{5,9},{6,10},{7,11},{8,12},{9,13},{1... | collective-permute-start | bytes 1843208 | tf_op jit(solution)/shard_map/ppermute | solution.py:32
  512.6 150.9 %collective-permute-start.7 = (bf16[80,3840]{1,0:T(8,128)(2,1)}, bf16[80,3840]{1,0:T(8,128)(2,1)S(1)}, u32[]{:S(2)}, u32[]{:S(2)}) collective-permute-start(bf16[80,3840]{1,0:T(8,128)(2,1)} %get-tuple-element.145), channel_id=1, source_target_pairs={{0,8},{1,9},{2,10},{3,11},{4,12},{5,13},{6,14},{7,15},{8,0},{9,1},... | collective-permute-start | bytes 1843208 | tf_op jit(solution)/shard_map/ppermute | solution.py:32
  513.1 150.4 %collective-permute-start.8 = (bf16[80,3840]{1,0:T(8,128)(2,1)}, bf16[80,3840]{1,0:T(8,128)(2,1)}, u32[]{:S(2)}, u32[]{:S(2)}) collective-permute-start(bf16[80,3840]{1,0:T(8,128)(2,1)} %get-tuple-element.146), channel_id=1, source_target_pairs={{0,12},{1,13},{2,14},{3,15},{4,0},{5,1},{6,2},{7,3},{8,4},{9,5},{1... | collective-permute-start | bytes 1843208 | tf_op jit(solution)/shard_map/ppermute | solution.py:32
  541.3 2.5 copy-start.2
  541.3 2.7 copy-start.10
  541.3 4.9 collective-permute-start.5
  544.0 15.4 %copy-start = (bf16[2560,512]{1,0:T(8,128)(2,1)}, bf16[2560,512]{1,0:T(8,128)(2,1)S(1)}, u32[]{:S(2)}) copy-start(bf16[2560,512]{1,0:T(8,128)(2,1)S(1)} %fusion) | copy-start | bytes 7864324
  658.5 11.5 %copy-start.7 = (bf16[4,32,2560]{2,1,0:T(8,128)(2,1)S(1)}, bf16[4,32,2560]{2,1,0:T(8,128)(2,1)}, u32[]{:S(2)}) copy-start(bf16[4,32,2560]{2,1,0:T(8,128)(2,1)} %get-tuple-element.112) | copy-start | bytes 1966084
  661.5 9.3 %copy-start.3 = (f32[4,32,2560]{2,1,0:T(8,128)S(1)}, f32[4,32,2560]{2,1,0:T(8,128)}, u32[]{:S(2)}) copy-start(f32[4,32,2560]{2,1,0:T(8,128)} %get-tuple-element.134) | copy-start | bytes 3932164
  663.5 0.8 copy-start.8
  663.5 1.0 copy-start.9

commit v2 on v1

--- a/solution.py
+++ b/solution.py
@@ -921,7 +921,7 @@
     stays = [
         pltpu.make_async_copy(mix_p.at[0], mix.slot(0, 0), local.at[0]),
         pltpu.make_async_copy(ffw_0, ffw.slot(0, 0), local.at[1]),
-        pltpu.make_async_copy(x_p, x_all.at[p.z, 0], local.at[2]),
+        pltpu.make_async_copy(x_p, x_all.at[p.z], local.at[2]),
         pltpu.make_async_copy(cot_p, cot_all.at[p.z, 0], local.at[3]),
     ]
     for copy in stays:
@@ -931,7 +931,8 @@
     for d in (1, 3):
         from_z(d, mix.slot(0, d))
         mix.spread(d)
-    line.begin(0, x_p)
+    for h in range(x_p.shape[0]):
+        line.begin(h, x_p.at[h])
     cot.begin(0, cot_p)
     from_z(2, mix.slot(0, 2))
     mix.spread(2)
@@ -939,17 +940,20 @@
     mix.sides(0)
     ffw.sides(0)
     mix.corner(0)
-    line.step(1, 0)
+    for h in range(x_p.shape[0]):
+        line.step(1, h)
     cot.step(1, 0)
     for d in (1, 3):
         mix.sides(d)
     ffw.corner(0)
-    line.step(2, 0)
+    for h in range(x_p.shape[0]):
+        line.step(2, h)
     cot.step(2, 0)
     for d in (1, 3):
         mix.corner(d)
     mix.sides(2)
-    line.step(3, 0)
+    for h in range(x_p.shape[0]):
+        line.step(3, h)
     cot.step(3, 0)
     mix.corner(2)
     from_z(0, piece_1)
@@ -957,7 +961,7 @@
     ffw.close((0,))
     for copy in started:
         copy.wait_send()
-    line.close(1)
+    line.close(x_p.shape[0])
     cot.close(1)
     for copy in stays:
         copy.wait()
@@ -973,13 +977,13 @@
             whole(mix_p),
             whole(ffw_0),
             jax.ShapeDtypeStruct(ffw_1.shape, BF),
-            jax.ShapeDtypeStruct((TP, 1) + x_p.shape, BF),
+            jax.ShapeDtypeStruct((TP,) + x_p.shape, BF),
             jax.ShapeDtypeStruct((TP, 1) + cot_p.shape, BF),
         ],
         scratch_shapes=[
             *pairs(TP),
-            *pairs(TP - 1, 1),
-            *pairs(TP - 1, 1),
+            *pairs(TP - 1, x_p.shape[0]),
+            *pairs(TP - 1, x_p.shape[0]),
             *pairs(TP - 1, 1),
             *pairs(TP - 1, 1),
             pltpu.SemaphoreType.DMA((4,)),
@@ -988,7 +992,7 @@
         ],
         compiler_params=pltpu.CompilerParams(collective_id=0, has_side_effects=True),
     )(mix_p, ffw_0, ffw_1, x_p, cot_p)
-    return mix_w.reshape(-1, mix_p.shape[-1]), ffw_w, piece_1, x_all[:, 0], cot_all
+    return mix_w.reshape(-1, mix_p.shape[-1]), ffw_w, piece_1, x_all, cot_all
 
 
 class Stream:
@@ -2026,7 +2030,7 @@
         weights = (proj_gelu, proj_lru, out_t, gate_blocks, small, ffw_gate, ffw_up, down_t)
         mix_pieces, ffw_pieces = pack(weights, block_width)
         mix_w, ffw_w, piece_1, x_all, cot_first = intake(
-            mix_pieces, ffw_pieces[0], ffw_pieces[1], x_wide, cot_halves[0], p
+            mix_pieces, ffw_pieces[0], ffw_pieces[1], x_wide.reshape(3, -1, width), cot_halves[0], p
         )
         piece_2, piece_3, x_all = lax.optimization_barrier((*ffw_pieces[2:], x_all))
         piece_3, piece_2 = shift_z(piece_3, 3), shift_z(piece_2, 2)

time: 679 us -> 676 us (level)
  no operation moved by 1% of the time
where the time goes in v2:
time: 676 us; the launch traced here: 669 us
  Pallas kernels  624 us (92%)
  starting transfers between devices  18.5 us (3%)
  local copies, waits for them, and re-layouts  16.2 us (2%)
    pallas_call x1, Pallas kernels, middle(): pl.pallas_call(functools.partial(middle_kernel, with_ffw), in_specs=[VMEM...  162 us
    pallas_call x1, Pallas kernels, turn(): pl.pallas_call(functools.partial(turn_kernel, count), in_specs=[VMEM] * 5...  150 us
    pallas_call x1, Pallas kernels, intake(): pl.pallas_call(intake_kernel, in_specs=[ANY] * 5, out_specs=[ANY] * 5, ou...  130 us
    pallas_call x1, Pallas kernels, final(): pl.pallas_call(final_kernel, in_specs=[VMEM] * 5 + [ANY] * 5, out_specs=[...  97.5 us
    pallas_call x1, Pallas kernels, recur(): pl.pallas_call(functools.partial(recur_kernel, dims), grid=(held,), in_sp...  16.6 us
    ppermute x7, starting transfers between devices, move(): return lax.ppermute(value, 'seq', pairs)  15.2 us
  transfers between devices with their start and end apart: 9, of which 3 were waited for; matrix products, arithmetic and copies ran while one was open for 2% of the time, Pallas kernels for 26%

profile of v2, /device:TPU:0, one launch (start us, length us, event | category | flops | bytes accessed | tf_op | source)
XLA Modules:
  0.0 668.8 jit_solution(8096604001474550383)
XLA Ops:
  1.6 2.4 collective-permute-start
  4.8 1.9 slice_bitcast_fusion
  7.3 5.2 shard_map.228
  13.5 130.1 %shard_map.229 = (bf16[2,1,4,2,2,80,2944]{6,5,4,3,2,1,0:T(8,128)(2,1)}, bf16[2,1,4,2,2,80,5760]{6,5,4,3,2,1,0:T(8,128)(2,1)}, bf16[80,5760]{1,0:T(8,128)(2,1)}, ...) custom-call(bf16[4,80,2944]{2,1,0:T(8,128)(2,1)} %get-tuple-element.86.mix_p, ...), custom_call_target="tpu_custom_call" | custom-call | tf_op jit(solution)/shard_map/pallas_call | solution.py:972
  143.6 1.5 collective-permute-start.1
  146.1 1.5 collective-permute-start.4
  147.5 16.6 %shard_map.230 = (f32[8,2560]{1,0:T(8,128)}, f32[8,768]{1,0:T(8,128)}, bf16[512,2560]{1,0:T(8,128)(2,1)}, f32[576,768]{1,0:T(8,128)}, f32[576,768]{1,0:T(8,128)}...) custom-call(bf16[576,2560]{1,0:T(8,128)(2,1)} %bitcast.64, ...), custom_call_target="tpu_custom_call" | custom-call | tf_op jit(solution)/shard_map/pallas_call | solution.py:325
  164.1 6.2 shard_map.231
  170.3 10.1 %shard_map.232 = (bf16[512,768]{1,0:T(8,128)(2,1)}, bf16[512,2560]{1,0:T(8,128)(2,1)}) custom-call(f32[576,768]{1,0:T(8,128)} %get-tuple-element.92.pre, f32[8,768]{1,0:T(8,128)} %get-tuple-element.93.rows, f32[512,768]{1,0:T(8,128)} %get-tuple-element.94.state, f32[512,768]{1,0:T(8,128)} %get-tuple-element.95.prod, f32[8,768]{1,0:T(8,128)} %get-tuple-element.97.start, ...), custom_call_target="tpu_custom_call" | custom-call | tf_op jit(solution)/shard_map/pallas_call | solution.py:386
  181.2 2.1 constant_dynamic-slice_fusion.1
  183.3 1.6 fusion.1
  184.9 3.0 collective-permute-done.3.refs_8_
  189.6 162.1 %shard_map.233 = (f32[4,32,2560]{2,1,0:T(8,128)}, bf16[4,4,32,2560]{3,2,1,0:T(8,128)(2,1)}, bf16[4,2,64,2560]{3,2,1,0:T(8,128)(2,1)}, bf16[2,1,4,2,2,80,5760]{6,...) custom-call(bf16[4,4,32,2560]{3,2,1,0:T(8,128)(2,1)} %bitcast.70, ...), custom_call_target="tpu_custom_call", output_to_operand_aliasing={{3}: (10, {})} | custom-call | tf_op jit(solution)/shard_map/pallas_call | solution.py:1286
  351.7 149.9 %shard_map.234 = (bf16[4,32,2560]{2,1,0:T(8,128)(2,1)}, f32[4,32,2560]{2,1,0:T(8,128)}, f32[8,2560]{1,0:T(8,128)}, bf16[4,4,32,2560]{3,2,1,0:T(8,128)(2,1)}, bf1...) custom-call(bf16[4,4,32,2560]{3,2,1,0:T(8,128)(2,1)} %bitcast.68, ...), custom_call_target="tpu_custom_call" | custom-call | tf_op jit(solution)/shard_map/pallas_call | solution.py:1662
  501.6 7.1 %collective-permute-start.6 = (bf16[80,3840]{1,0:T(8,128)(2,1)}, bf16[80,3840]{1,0:T(8,128)(2,1)S(1)}, u32[]{:S(2)}, u32[]{:S(2)}) collective-permute-start(bf16[80,3840]{1,0:T(8,128)(2,1)} %get-tuple-element.144), channel_id=1, source_target_pairs={{0,4},{1,5},{2,6},{3,7},{4,8},{5,9},{6,10},{7,11},{8,12},{9,13},{1... | collective-permute-start | bytes 1843208 | tf_op jit(solution)/shard_map/ppermute | solution.py:32
  509.6 2.8 collective-permute-start.8
  512.5 10.4 %shard_map.235 = (bf16[512,768]{1,0:T(8,128)(2,1)}, f32[512,768]{1,0:T(8,128)}, f32[512,768]{1,0:T(8,128)}, f32[8,768]{1,0:T(8,128)}) custom-call(bf16[512,2560]{1,0:T(8,128)(2,1)} %bitcast.56, f32[576,768]{1,0:T(8,128)} %get-tuple-element.92.pre, f32[8,768]{1,0:T(8,128)} %get-tuple-element.93.rows, f32[512,768]{1,0:T(8,128)} %get-tuple-element.94.state, ...), custom_call_target="tpu_custom_call" | custom-call | tf_op jit(solution)/shard_map/pallas_call | solution.py:427
  522.8 5.6 shard_map.236
  528.5 9.4 %shard_map.237 = (f32[768,512]{1,0:T(8,128)}, f32[512,768]{1,0:T(8,128)}, f32[64,768]{1,0:T(8,128)}, f32[8,768]{1,0:T(8,128)}) custom-call(f32[512,768]{1,0:T(8,128)} %get-tuple-element.116.local, f32[512,768]{1,0:T(8,128)} %get-tuple-element.117.prods, f32[8,768]{1,0:T(8,128)} %get-tuple-element.120.carried, f32[512,768]{1,0:T(8,128)} %get-tuple-element.94.state, ...), custom_call_target="tpu_custom_call" | custom-call | tf_op jit(solution)/shard_map/pallas_call | solution.py:501
  540.6 2.2 collective-permute-done.5
  543.5 12.4 %shard_map.238 = (bf16[512,1536]{1,0:T(8,128)(2,1)}, bf16[512,2560]{1,0:T(8,128)(2,1)}, f32[8,2560]{1,0:T(8,128)}) custom-call(bf16[512,768]{1,0:T(8,128)(2,1)} %get-tuple-element.115.gelu, f32[512,768]{1,0:T(8,128)} %get-tuple-element.123.lru, f32[64,768]{1,0:T(8,128)} %bitcast.73, f32[8,768]{1,0:T(8,128)} %get-tuple-element.93.rows, ...), custom_call_target="tpu_custom_call" | custom-call | tf_op jit(solution)/shard_map/pallas_call | solution.py:565
  557.5 97.5 %shard_map.239 = (f32[4,32,2560]{2,1,0:T(8,128)}, f32[8,2560]{1,0:T(8,128)}, bf16[4,80,512]{2,1,0:T(8,128)(2,1)}, bf16[4,80,768]{2,1,0:T(8,128)(2,1)}, bf16[4,80...) custom-call(bf16[4,4,32,2560]{3,2,1,0:T(8,128)(2,1)} %bitcast.69, ...), custom_call_target="tpu_custom_call" | custom-call | tf_op jit(solution)/shard_map/pallas_call | solution.py:1834
  655.0 3.0 shard_map.240
  661.0 5.5 shard_map.241
  (54 shorter events, 17.5 us)
Async XLA Ops:
  1.6 10.9 %collective-permute-start = (bf16[2,3,2560]{2,1,0:T(4,128)(2,1)S(1)}, bf16[2,3,2560]{2,1,0:T(4,128)(2,1)S(1)}, u32[]{:S(2)}, u32[]{:S(2)}) collective-permute-start(bf16[2,3,2560]{2,1,0:T(4,128)(2,1)S(1)} %slice.58), channel_id=1, source_target_pairs={{0,1},{1,2},{2,3},{3,4},{4,5},{5,6},{6,7},{7,8},{8,9},{9,10},{10,1... | collective-permute-start | bytes 92168 | tf_op jit(solution)/shard_map/ppermute | solution.py:2022
  7.3 5.2 copy-start.1
  143.6 44.8 %collective-permute-start.1 = (bf16[80,5760]{1,0:T(8,128)(2,1)}, bf16[80,5760]{1,0:T(8,128)(2,1)S(1)}, u32[]{:S(2)}, u32[]{:S(2)}) collective-permute-start(bf16[80,5760]{1,0:T(8,128)(2,1)} %get-tuple-element.101.refs_5_), channel_id=1, source_target_pairs={{0,2},{1,3},{2,0},{3,1},{4,6},{5,7},{6,4},{7,5},{8,10},{9,11},{10,... | collective-permute-start | bytes 2764808 | tf_op jit(solution)/shard_map/ppermute | solution.py:32
  145.1 43.3 %collective-permute-start.2 = (bf16[80,5760]{1,0:T(8,128)(2,1)}, bf16[80,5760]{1,0:T(8,128)(2,1)S(1)}, u32[]{:S(2)}, u32[]{:S(2)}) collective-permute-start(bf16[80,5760]{1,0:T(8,128)(2,1)} %get-tuple-element.101.refs_5_), channel_id=1, source_target_pairs={{0,16},{16,0},{1,17},{17,1},{2,18},{18,2},{3,19},{19,3},{4,20},{20... | collective-permute-start | bytes 2764808 | tf_op jit(solution)/shard_map/ppermute | solution.py:44
  146.1 41.8 %collective-permute-start.3 = (bf16[80,5760]{1,0:T(8,128)(2,1)}, bf16[80,5760]{1,0:T(8,128)(2,1)S(1)}, u32[]{:S(2)}, u32[]{:S(2)}) collective-permute-start(bf16[80,5760]{1,0:T(8,128)(2,1)} %get-tuple-element.102), channel_id=1, source_target_pairs={{0,8},{1,9},{2,10},{3,11},{4,12},{5,13},{6,14},{7,15},{8,0},{9,1},... | collective-permute-start | bytes 2764808 | tf_op jit(solution)/shard_map/ppermute | solution.py:32
  146.1 42.3 %collective-permute-start.4 = (bf16[80,5760]{1,0:T(8,128)(2,1)}, bf16[80,5760]{1,0:T(8,128)(2,1)}, u32[]{:S(2)}, u32[]{:S(2)}) collective-permute-start(bf16[80,5760]{1,0:T(8,128)(2,1)} %get-tuple-element.103), channel_id=1, source_target_pairs={{0,12},{1,13},{2,14},{3,15},{4,0},{5,1},{6,2},{7,3},{8,4},{9,5},{1... | collective-permute-start | bytes 2764808 | tf_op jit(solution)/shard_map/ppermute | solution.py:32
  187.9 0.9 copy-start.6
  188.4 0.9 copy-start.4
  188.4 1.2 copy-start.5
  501.6 158.4 %collective-permute-start.6 = (bf16[80,3840]{1,0:T(8,128)(2,1)}, bf16[80,3840]{1,0:T(8,128)(2,1)S(1)}, u32[]{:S(2)}, u32[]{:S(2)}) collective-permute-start(bf16[80,3840]{1,0:T(8,128)(2,1)} %get-tuple-element.144), channel_id=1, source_target_pairs={{0,4},{1,5},{2,6},{3,7},{4,8},{5,9},{6,10},{7,11},{8,12},{9,13},{1... | collective-permute-start | bytes 1843208 | tf_op jit(solution)/shard_map/ppermute | solution.py:32
  508.7 151.3 %collective-permute-start.7 = (bf16[80,3840]{1,0:T(8,128)(2,1)}, bf16[80,3840]{1,0:T(8,128)(2,1)S(1)}, u32[]{:S(2)}, u32[]{:S(2)}) collective-permute-start(bf16[80,3840]{1,0:T(8,128)(2,1)} %get-tuple-element.145), channel_id=1, source_target_pairs={{0,8},{1,9},{2,10},{3,11},{4,12},{5,13},{6,14},{7,15},{8,0},{9,1},... | collective-permute-start | bytes 1843208 | tf_op jit(solution)/shard_map/ppermute | solution.py:32
  509.6 150.4 %collective-permute-start.8 = (bf16[80,3840]{1,0:T(8,128)(2,1)}, bf16[80,3840]{1,0:T(8,128)(2,1)}, u32[]{:S(2)}, u32[]{:S(2)}) collective-permute-start(bf16[80,3840]{1,0:T(8,128)(2,1)} %get-tuple-element.146), channel_id=1, source_target_pairs={{0,12},{1,13},{2,14},{3,15},{4,0},{5,1},{6,2},{7,3},{8,4},{9,5},{1... | collective-permute-start | bytes 1843208 | tf_op jit(solution)/shard_map/ppermute | solution.py:32
  537.8 2.5 copy-start.2
  537.8 2.7 copy-start.10
  537.9 4.9 collective-permute-start.5
  540.5 15.4 %copy-start = (bf16[2560,512]{1,0:T(8,128)(2,1)}, bf16[2560,512]{1,0:T(8,128)(2,1)S(1)}, u32[]{:S(2)}) copy-start(bf16[2560,512]{1,0:T(8,128)(2,1)S(1)} %fusion) | copy-start | bytes 7864324
  655.0 11.5 %copy-start.7 = (bf16[4,32,2560]{2,1,0:T(8,128)(2,1)S(1)}, bf16[4,32,2560]{2,1,0:T(8,128)(2,1)}, u32[]{:S(2)}) copy-start(bf16[4,32,2560]{2,1,0:T(8,128)(2,1)} %get-tuple-element.112) | copy-start | bytes 1966084
  658.0 9.3 %copy-start.3 = (f32[4,32,2560]{2,1,0:T(8,128)S(1)}, f32[4,32,2560]{2,1,0:T(8,128)}, u32[]{:S(2)}) copy-start(f32[4,32,2560]{2,1,0:T(8,128)} %get-tuple-element.134) | copy-start | bytes 3932164
  660.0 0.8 copy-start.8
  660.0 1.0 copy-start.9

commit v3 on v2

--- a/solution.py
+++ b/solution.py
@@ -922,7 +922,7 @@
         pltpu.make_async_copy(mix_p.at[0], mix.slot(0, 0), local.at[0]),
         pltpu.make_async_copy(ffw_0, ffw.slot(0, 0), local.at[1]),
         pltpu.make_async_copy(x_p, x_all.at[p.z], local.at[2]),
-        pltpu.make_async_copy(cot_p, cot_all.at[p.z, 0], local.at[3]),
+        pltpu.make_async_copy(cot_p, cot_all.at[p.z], local.at[3]),
     ]
     for copy in stays:
         copy.start()
@@ -933,7 +933,8 @@
         mix.spread(d)
     for h in range(x_p.shape[0]):
         line.begin(h, x_p.at[h])
-    cot.begin(0, cot_p)
+    for h in range(cot_p.shape[0]):
+        cot.begin(h, cot_p.at[h])
     from_z(2, mix.slot(0, 2))
     mix.spread(2)
     along_z(0, ffw_1, piece_1, 1)
@@ -942,19 +943,22 @@
     mix.corner(0)
     for h in range(x_p.shape[0]):
         line.step(1, h)
-    cot.step(1, 0)
+    for h in range(cot_p.shape[0]):
+        cot.step(1, h)
     for d in (1, 3):
         mix.sides(d)
     ffw.corner(0)
     for h in range(x_p.shape[0]):
         line.step(2, h)
-    cot.step(2, 0)
+    for h in range(cot_p.shape[0]):
+        cot.step(2, h)
     for d in (1, 3):
         mix.corner(d)
     mix.sides(2)
     for h in range(x_p.shape[0]):
         line.step(3, h)
-    cot.step(3, 0)
+    for h in range(cot_p.shape[0]):
+        cot.step(3, h)
     mix.corner(2)
     from_z(0, piece_1)
     mix.close(range(TP))
@@ -962,7 +966,7 @@
     for copy in started:
         copy.wait_send()
     line.close(x_p.shape[0])
-    cot.close(1)
+    cot.close(cot_p.shape[0])
     for copy in stays:
         copy.wait()
 
@@ -978,21 +982,21 @@
             whole(ffw_0),
             jax.ShapeDtypeStruct(ffw_1.shape, BF),
             jax.ShapeDtypeStruct((TP,) + x_p.shape, BF),
-            jax.ShapeDtypeStruct((TP, 1) + cot_p.shape, BF),
+            jax.ShapeDtypeStruct((TP,) + cot_p.shape, BF),
         ],
         scratch_shapes=[
             *pairs(TP),
             *pairs(TP - 1, x_p.shape[0]),
             *pairs(TP - 1, x_p.shape[0]),
-            *pairs(TP - 1, 1),
-            *pairs(TP - 1, 1),
+            *pairs(TP - 1, cot_p.shape[0]),
+            *pairs(TP - 1, cot_p.shape[0]),
             pltpu.SemaphoreType.DMA((4,)),
             *Spread.scratch(),
             *Spread.scratch(),
         ],
         compiler_params=pltpu.CompilerParams(collective_id=0, has_side_effects=True),
     )(mix_p, ffw_0, ffw_1, x_p, cot_p)
-    return mix_w.reshape(-1, mix_p.shape[-1]), ffw_w, piece_1, x_all, cot_all
+    return mix_w.reshape(-1, mix_p.shape[-1]), ffw_w, piece_1, x_all, cot_all.reshape(TP, 1, -1, cot_p.shape[-1])
 
 
 class Stream:
@@ -2030,7 +2034,7 @@
         weights = (proj_gelu, proj_lru, out_t, gate_blocks, small, ffw_gate, ffw_up, down_t)
         mix_pieces, ffw_pieces = pack(weights, block_width)
         mix_w, ffw_w, piece_1, x_all, cot_first = intake(
-            mix_pieces, ffw_pieces[0], ffw_pieces[1], x_wide.reshape(3, -1, width), cot_halves[0], p
+            mix_pieces, ffw_pieces[0], ffw_pieces[1], x_wide.reshape(3, -1, width), cot_halves[0].reshape(2, -1, width), p
         )
         piece_2, piece_3, x_all = lax.optimization_barrier((*ffw_pieces[2:], x_all))
         piece_3, piece_2 = shift_z(piece_3, 3), shift_z(piece_2, 2)

time: 676 us -> 676 us (level)
  no operation moved by 1% of the time
where the time goes in v3:
time: 676 us; the launch traced here: 669 us
  Pallas kernels  624 us (92%)
  starting transfers between devices  18.5 us (3%)
  local copies, waits for them, and re-layouts  16.2 us (2%)
    pallas_call x1, Pallas kernels, middle(): pl.pallas_call(functools.partial(middle_kernel, with_ffw), in_specs=[VMEM...  162 us
    pallas_call x1, Pallas kernels, turn(): pl.pallas_call(functools.partial(turn_kernel, count), in_specs=[VMEM] * 5...  150 us
    pallas_call x1, Pallas kernels, intake(): pl.pallas_call(intake_kernel, in_specs=[ANY] * 5, out_specs=[ANY] * 5, ou...  130 us
    pallas_call x1, Pallas kernels, final(): pl.pallas_call(final_kernel, in_specs=[VMEM] * 5 + [ANY] * 5, out_specs=[...  97.5 us
    pallas_call x1, Pallas kernels, recur(): pl.pallas_call(functools.partial(recur_kernel, dims), grid=(held,), in_sp...  16.6 us
    ppermute x7, starting transfers between devices, move(): return lax.ppermute(value, 'seq', pairs)  15.2 us
  transfers between devices with their start and end apart: 9, of which 3 were waited for; matrix products, arithmetic and copies ran while one was open for 2% of the time, Pallas kernels for 26%

profile of v3, /device:TPU:0, one launch (start us, length us, event | category | flops | bytes accessed | tf_op | source)
XLA Modules:
  0.0 668.9 jit_solution(4885927665224957966)
XLA Ops:
  1.6 2.4 collective-permute-start
  4.8 1.9 slice_bitcast_fusion
  7.3 5.2 shard_map.228
  13.5 130.2 %shard_map.229 = (bf16[2,1,4,2,2,80,2944]{6,5,4,3,2,1,0:T(8,128)(2,1)}, bf16[2,1,4,2,2,80,5760]{6,5,4,3,2,1,0:T(8,128)(2,1)}, bf16[80,5760]{1,0:T(8,128)(2,1)}, ...) custom-call(bf16[4,80,2944]{2,1,0:T(8,128)(2,1)} %get-tuple-element.86.mix_p, ...), custom_call_target="tpu_custom_call" | custom-call | tf_op jit(solution)/shard_map/pallas_call | solution.py:976
  143.7 1.5 collective-permute-start.1
  146.2 1.5 collective-permute-start.4
  147.7 16.6 %shard_map.230 = (f32[8,2560]{1,0:T(8,128)}, f32[8,768]{1,0:T(8,128)}, bf16[512,2560]{1,0:T(8,128)(2,1)}, f32[576,768]{1,0:T(8,128)}, f32[576,768]{1,0:T(8,128)}...) custom-call(bf16[576,2560]{1,0:T(8,128)(2,1)} %bitcast.64, ...), custom_call_target="tpu_custom_call" | custom-call | tf_op jit(solution)/shard_map/pallas_call | solution.py:325
  164.2 6.2 shard_map.231
  170.4 10.1 %shard_map.232 = (bf16[512,768]{1,0:T(8,128)(2,1)}, bf16[512,2560]{1,0:T(8,128)(2,1)}) custom-call(f32[576,768]{1,0:T(8,128)} %get-tuple-element.92.pre, f32[8,768]{1,0:T(8,128)} %get-tuple-element.93.rows, f32[512,768]{1,0:T(8,128)} %get-tuple-element.94.state, f32[512,768]{1,0:T(8,128)} %get-tuple-element.95.prod, f32[8,768]{1,0:T(8,128)} %get-tuple-element.97.start, ...), custom_call_target="tpu_custom_call" | custom-call | tf_op jit(solution)/shard_map/pallas_call | solution.py:386
  181.3 2.1 constant_dynamic-slice_fusion.1
  183.5 1.6 fusion.1
  185.0 3.0 collective-permute-done.3.refs_8_
  189.7 162.2 %shard_map.233 = (f32[4,32,2560]{2,1,0:T(8,128)}, bf16[4,4,32,2560]{3,2,1,0:T(8,128)(2,1)}, bf16[4,2,64,2560]{3,2,1,0:T(8,128)(2,1)}, bf16[2,1,4,2,2,80,5760]{6,...) custom-call(bf16[4,4,32,2560]{3,2,1,0:T(8,128)(2,1)} %bitcast.70, ...), custom_call_target="tpu_custom_call", output_to_operand_aliasing={{3}: (10, {})} | custom-call | tf_op jit(solution)/shard_map/pallas_call | solution.py:1290
  351.9 149.9 %shard_map.234 = (bf16[4,32,2560]{2,1,0:T(8,128)(2,1)}, f32[4,32,2560]{2,1,0:T(8,128)}, f32[8,2560]{1,0:T(8,128)}, bf16[4,4,32,2560]{3,2,1,0:T(8,128)(2,1)}, bf1...) custom-call(bf16[4,4,32,2560]{3,2,1,0:T(8,128)(2,1)} %bitcast.68, ...), custom_call_target="tpu_custom_call" | custom-call | tf_op jit(solution)/shard_map/pallas_call | solution.py:1666
  501.8 7.1 %collective-permute-start.6 = (bf16[80,3840]{1,0:T(8,128)(2,1)}, bf16[80,3840]{1,0:T(8,128)(2,1)S(1)}, u32[]{:S(2)}, u32[]{:S(2)}) collective-permute-start(bf16[80,3840]{1,0:T(8,128)(2,1)} %get-tuple-element.144), channel_id=1, source_target_pairs={{0,4},{1,5},{2,6},{3,7},{4,8},{5,9},{6,10},{7,11},{8,12},{9,13},{1... | collective-permute-start | bytes 1843208 | tf_op jit(solution)/shard_map/ppermute | solution.py:32
  509.7 2.8 collective-permute-start.8
  512.6 10.4 %shard_map.235 = (bf16[512,768]{1,0:T(8,128)(2,1)}, f32[512,768]{1,0:T(8,128)}, f32[512,768]{1,0:T(8,128)}, f32[8,768]{1,0:T(8,128)}) custom-call(bf16[512,2560]{1,0:T(8,128)(2,1)} %bitcast.56, f32[576,768]{1,0:T(8,128)} %get-tuple-element.92.pre, f32[8,768]{1,0:T(8,128)} %get-tuple-element.93.rows, f32[512,768]{1,0:T(8,128)} %get-tuple-element.94.state, ...), custom_call_target="tpu_custom_call" | custom-call | tf_op jit(solution)/shard_map/pallas_call | solution.py:427
  523.0 5.6 shard_map.236
  528.6 9.4 %shard_map.237 = (f32[768,512]{1,0:T(8,128)}, f32[512,768]{1,0:T(8,128)}, f32[64,768]{1,0:T(8,128)}, f32[8,768]{1,0:T(8,128)}) custom-call(f32[512,768]{1,0:T(8,128)} %get-tuple-element.116.local, f32[512,768]{1,0:T(8,128)} %get-tuple-element.117.prods, f32[8,768]{1,0:T(8,128)} %get-tuple-element.120.carried, f32[512,768]{1,0:T(8,128)} %get-tuple-element.94.state, ...), custom_call_target="tpu_custom_call" | custom-call | tf_op jit(solution)/shard_map/pallas_call | solution.py:501
  540.7 2.2 collective-permute-done.5
  543.6 12.4 %shard_map.238 = (bf16[512,1536]{1,0:T(8,128)(2,1)}, bf16[512,2560]{1,0:T(8,128)(2,1)}, f32[8,2560]{1,0:T(8,128)}) custom-call(bf16[512,768]{1,0:T(8,128)(2,1)} %get-tuple-element.115.gelu, f32[512,768]{1,0:T(8,128)} %get-tuple-element.123.lru, f32[64,768]{1,0:T(8,128)} %bitcast.75, f32[8,768]{1,0:T(8,128)} %get-tuple-element.93.rows, ...), custom_call_target="tpu_custom_call" | custom-call | tf_op jit(solution)/shard_map/pallas_call | solution.py:565
  557.6 97.5 %shard_map.239 = (f32[4,32,2560]{2,1,0:T(8,128)}, f32[8,2560]{1,0:T(8,128)}, bf16[4,80,512]{2,1,0:T(8,128)(2,1)}, bf16[4,80,768]{2,1,0:T(8,128)(2,1)}, bf16[4,80...) custom-call(bf16[4,4,32,2560]{3,2,1,0:T(8,128)(2,1)} %bitcast.69, ...), custom_call_target="tpu_custom_call" | custom-call | tf_op jit(solution)/shard_map/pallas_call | solution.py:1838
  655.1 3.0 shard_map.240
  661.1 5.5 shard_map.241
  (54 shorter events, 17.5 us)
Async XLA Ops:
  1.6 10.9 %collective-permute-start = (bf16[2,3,2560]{2,1,0:T(4,128)(2,1)S(1)}, bf16[2,3,2560]{2,1,0:T(4,128)(2,1)S(1)}, u32[]{:S(2)}, u32[]{:S(2)}) collective-permute-start(bf16[2,3,2560]{2,1,0:T(4,128)(2,1)S(1)} %slice.58), channel_id=1, source_target_pairs={{0,1},{1,2},{2,3},{3,4},{4,5},{5,6},{6,7},{7,8},{8,9},{9,10},{10,1... | collective-permute-start | bytes 92168 | tf_op jit(solution)/shard_map/ppermute | solution.py:2026
  7.3 5.2 copy-start.1
  143.7 44.8 %collective-permute-start.1 = (bf16[80,5760]{1,0:T(8,128)(2,1)}, bf16[80,5760]{1,0:T(8,128)(2,1)S(1)}, u32[]{:S(2)}, u32[]{:S(2)}) collective-permute-start(bf16[80,5760]{1,0:T(8,128)(2,1)} %get-tuple-element.101.refs_5_), channel_id=1, source_target_pairs={{0,2},{1,3},{2,0},{3,1},{4,6},{5,7},{6,4},{7,5},{8,10},{9,11},{10,... | collective-permute-start | bytes 2764808 | tf_op jit(solution)/shard_map/ppermute | solution.py:32
  145.2 43.3 %collective-permute-start.2 = (bf16[80,5760]{1,0:T(8,128)(2,1)}, bf16[80,5760]{1,0:T(8,128)(2,1)S(1)}, u32[]{:S(2)}, u32[]{:S(2)}) collective-permute-start(bf16[80,5760]{1,0:T(8,128)(2,1)} %get-tuple-element.101.refs_5_), channel_id=1, source_target_pairs={{0,16},{16,0},{1,17},{17,1},{2,18},{18,2},{3,19},{19,3},{4,20},{20... | collective-permute-start | bytes 2764808 | tf_op jit(solution)/shard_map/ppermute | solution.py:44
  146.2 41.8 %collective-permute-start.3 = (bf16[80,5760]{1,0:T(8,128)(2,1)}, bf16[80,5760]{1,0:T(8,128)(2,1)S(1)}, u32[]{:S(2)}, u32[]{:S(2)}) collective-permute-start(bf16[80,5760]{1,0:T(8,128)(2,1)} %get-tuple-element.102), channel_id=1, source_target_pairs={{0,8},{1,9},{2,10},{3,11},{4,12},{5,13},{6,14},{7,15},{8,0},{9,1},... | collective-permute-start | bytes 2764808 | tf_op jit(solution)/shard_map/ppermute | solution.py:32
  146.2 42.3 %collective-permute-start.4 = (bf16[80,5760]{1,0:T(8,128)(2,1)}, bf16[80,5760]{1,0:T(8,128)(2,1)}, u32[]{:S(2)}, u32[]{:S(2)}) collective-permute-start(bf16[80,5760]{1,0:T(8,128)(2,1)} %get-tuple-element.103), channel_id=1, source_target_pairs={{0,12},{1,13},{2,14},{3,15},{4,0},{5,1},{6,2},{7,3},{8,4},{9,5},{1... | collective-permute-start | bytes 2764808 | tf_op jit(solution)/shard_map/ppermute | solution.py:32
  188.0 0.9 copy-start.6
  188.5 0.9 copy-start.4
  188.5 1.2 copy-start.5
  501.8 158.4 %collective-permute-start.6 = (bf16[80,3840]{1,0:T(8,128)(2,1)}, bf16[80,3840]{1,0:T(8,128)(2,1)S(1)}, u32[]{:S(2)}, u32[]{:S(2)}) collective-permute-start(bf16[80,3840]{1,0:T(8,128)(2,1)} %get-tuple-element.144), channel_id=1, source_target_pairs={{0,4},{1,5},{2,6},{3,7},{4,8},{5,9},{6,10},{7,11},{8,12},{9,13},{1... | collective-permute-start | bytes 1843208 | tf_op jit(solution)/shard_map/ppermute | solution.py:32
  508.8 151.3 %collective-permute-start.7 = (bf16[80,3840]{1,0:T(8,128)(2,1)}, bf16[80,3840]{1,0:T(8,128)(2,1)S(1)}, u32[]{:S(2)}, u32[]{:S(2)}) collective-permute-start(bf16[80,3840]{1,0:T(8,128)(2,1)} %get-tuple-element.145), channel_id=1, source_target_pairs={{0,8},{1,9},{2,10},{3,11},{4,12},{5,13},{6,14},{7,15},{8,0},{9,1},... | collective-permute-start | bytes 1843208 | tf_op jit(solution)/shard_map/ppermute | solution.py:32
  509.7 150.4 %collective-permute-start.8 = (bf16[80,3840]{1,0:T(8,128)(2,1)}, bf16[80,3840]{1,0:T(8,128)(2,1)}, u32[]{:S(2)}, u32[]{:S(2)}) collective-permute-start(bf16[80,3840]{1,0:T(8,128)(2,1)} %get-tuple-element.146), channel_id=1, source_target_pairs={{0,12},{1,13},{2,14},{3,15},{4,0},{5,1},{6,2},{7,3},{8,4},{9,5},{1... | collective-permute-start | bytes 1843208 | tf_op jit(solution)/shard_map/ppermute | solution.py:32
  538.0 2.5 copy-start.2
  538.0 2.7 copy-start.10
  538.0 4.9 collective-permute-start.5
  540.6 15.4 %copy-start = (bf16[2560,512]{1,0:T(8,128)(2,1)}, bf16[2560,512]{1,0:T(8,128)(2,1)S(1)}, u32[]{:S(2)}) copy-start(bf16[2560,512]{1,0:T(8,128)(2,1)S(1)} %fusion) | copy-start | bytes 7864324
  655.1 11.5 %copy-start.7 = (bf16[4,32,2560]{2,1,0:T(8,128)(2,1)S(1)}, bf16[4,32,2560]{2,1,0:T(8,128)(2,1)}, u32[]{:S(2)}) copy-start(bf16[4,32,2560]{2,1,0:T(8,128)(2,1)} %get-tuple-element.112) | copy-start | bytes 1966084
  658.1 9.3 %copy-start.3 = (f32[4,32,2560]{2,1,0:T(8,128)S(1)}, f32[4,32,2560]{2,1,0:T(8,128)}, u32[]{:S(2)}) copy-start(f32[4,32,2560]{2,1,0:T(8,128)} %get-tuple-element.134) | copy-start | bytes 3932164
  660.1 0.8 copy-start.8
  660.1 1.0 copy-start.9
